TPU v7x, 256 devices: a whole 4x4x8 slice. The times are simulated.
256 devices in a mesh: ctx: 32 (over y, x, core), exp: 8 (over z).
Axes of the slice: x: 4, y: 4, z: 8, core: 2. Of those that a mesh axis runs over, the one named last changes fastest.
Arguments:
- query: bfloat16 [2048, 4096], P('ctx', 'exp'), may hold values from -24 to 24
- key_states: bfloat16 [2048, 1024], P('ctx', 'exp'), may hold values from -24 to 24
- value_states: bfloat16 [2048, 1024], P('ctx', 'exp'), may hold values from -6 to 6
- residual: bfloat16 [2048, 4096], P('ctx'), may hold values from -6 to 6
- out_weight: bfloat16 [4096, 4096], P('exp'), may hold values from -0.09375 to 0.09375
- norm_gain: float32 [4096], replicated, may hold values from 0.1 to 1.9
- router_weight: bfloat16 [4096, 8], replicated, may hold values from -0.1875 to 0.1875
- expert_ids: int32 [2048, 2], P('ctx'), may hold values from 0 to 7, all different within a row; in each aligned block of 64 rows (0 to 63, 64 to 127, ...) at most 20 rows name the same one
- gate_weight: bfloat16 [8, 4096, 7168], P('exp', None, 'ctx'), may hold values from -0.09375 to 0.09375
- up_weight: bfloat16 [8, 4096, 7168], P('exp', None, 'ctx'), may hold values from -0.09375 to 0.09375
- down_weight: bfloat16 [8, 7168, 4096], P('exp', 'ctx'), may hold values from -0.0625 to 0.0625
Outputs:
- attended: bfloat16 [2048, 4096], P('ctx')
- expert_mix: bfloat16 [2048, 4096], P('ctx', 'exp')
Inputs may be any that keep to these rules, and one draw needn't show every extreme that they name: `expert_ids`: in each aligned block of 64 rows (the tokens of one context shard) no expert is named by more than 20 rows, a bound that some block reaches; the two entries of a row differ.
All inputs are finite; a program needn't handle non-finite values.
Results may differ from a plain program's by a relative error of at most 0.034.
Values may be sent and summed in bfloat16 or wider, within the bound.
A program may use at most 64 MiB of HBM per device.

v0:
```python
import math

import jax
import jax.numpy as jnp
from jax import lax
from jax.sharding import PartitionSpec as P

WINDOW = 4096


def local(
    query,
    key_states,
    value_states,
    residual,
    out_weight,
    norm_gain,
    router_weight,
    expert_ids,
    gate_weight,
    up_weight,
    down_weight,
):
    tokens = query.shape[0]
    head_dim = key_states.shape[1]
    groups = query.shape[1] // head_dim
    top_count = expert_ids.shape[1]
    ctx_index = lax.axis_index("ctx")
    exp_index = lax.axis_index("exp")
    exp_count = lax.axis_size("exp")
    score_scale = 1.0 / math.sqrt(head_dim)
    queries = query.reshape(tokens, groups, head_dim)
    query_pos = ctx_index * tokens + jnp.arange(tokens, dtype=jnp.int32)
    key_value = jnp.stack([key_states, value_states])
    block_rows = lax.all_gather(key_value, "ctx", axis=1, tiled=True)
    largest = jnp.full((tokens, groups), -1e30, jnp.float32)
    key_rows = block_rows[0]
    value_rows = block_rows[1]
    row_count = key_rows.shape[0]
    scores = (
        jnp.einsum("tgd,sd->tgs", queries, key_rows, preferred_element_type=jnp.float32)
        * score_scale
    )
    key_pos = jnp.arange(row_count, dtype=jnp.int32)
    allowed = (
        (key_pos[None, :] <= query_pos[:, None])
        & (key_pos[None, :] > query_pos[:, None] - WINDOW)
        & (key_pos[None, :] >= 0)
    )
    allowed = allowed[:, None, :]
    new_max = jnp.maximum(largest, jnp.max(jnp.where(allowed, scores, -1e30), axis=-1))
    weights = jnp.where(allowed, jnp.exp(scores - new_max[..., None]), 0.0)
    weight_sum = jnp.sum(weights, axis=-1)
    accumulated = jnp.einsum(
        "tgs,sd->tgd", weights.astype(jnp.bfloat16), value_rows, preferred_element_type=jnp.float32
    )
    running = (new_max, weight_sum, accumulated)
    largest, weight_sum, accumulated = running
    attention = (
        (accumulated / weight_sum[..., None])
        .astype(jnp.bfloat16)
        .reshape(tokens, groups * head_dim)
    )
    projected = jnp.dot(attention, out_weight, preferred_element_type=jnp.float32)
    attended = residual.astype(jnp.float32) + lax.psum(
        projected.astype(jnp.bfloat16), "exp"
    ).astype(jnp.float32)
    mean_square = jnp.mean(attended * attended, axis=-1, keepdims=True)
    normed = (attended * lax.rsqrt(mean_square + 1e-05) * norm_gain).astype(jnp.bfloat16)
    logits = jnp.dot(normed, router_weight, preferred_element_type=jnp.float32)
    chosen = jnp.take_along_axis(logits, expert_ids, axis=1)
    first_gate = jax.nn.sigmoid(chosen[:, 0] - chosen[:, 1])
    gate_probs = jnp.stack([first_gate, 1.0 - first_gate], axis=1)
    flat_ids = expert_ids.reshape(-1)
    one_hot = (flat_ids[:, None] == jnp.arange(exp_count, dtype=jnp.int32)[None, :]).astype(
        jnp.int32
    )
    earlier = jnp.cumsum(one_hot, axis=0) - one_hot
    slot_index = jnp.sum(earlier * one_hot, axis=-1)
    capacity = tokens * top_count * 5 // (4 * exp_count)
    is_mine = flat_ids == exp_index
    placing = (
        (slot_index[None, :] == jnp.arange(capacity, dtype=jnp.int32)[:, None]) & is_mine[None, :]
    ).astype(jnp.bfloat16)
    source = jnp.repeat(normed, top_count, axis=0)
    buffer = jnp.dot(placing, source, preferred_element_type=jnp.float32).astype(jnp.bfloat16)
    block_rows = lax.all_gather(buffer, "ctx", axis=0, tiled=True)
    gate = jnp.dot(block_rows, gate_weight[0], preferred_element_type=jnp.float32)
    upward = jnp.dot(block_rows, up_weight[0], preferred_element_type=jnp.float32)
    hidden = (jax.nn.silu(gate) * upward).astype(jnp.bfloat16)
    results = lax.psum_scatter(
        jnp.dot(hidden, down_weight[0], preferred_element_type=jnp.float32).astype(jnp.bfloat16),
        "ctx",
        scatter_dimension=0,
        tiled=True,
    ).astype(jnp.float32)
    token_slots = slot_index.reshape(tokens, top_count)
    contribution = jnp.zeros((tokens, results.shape[1]), jnp.float32)
    for which in range(top_count):
        selected = expert_ids[:, which] == exp_index
        picked = jnp.take(results, jnp.clip(token_slots[:, which], 0, capacity - 1), axis=0)
        contribution = (
            contribution + picked * jnp.where(selected, gate_probs[:, which], 0.0)[:, None]
        )
    mixture = lax.psum_scatter(
        contribution.astype(jnp.bfloat16), "exp", scatter_dimension=1, tiled=True
    )
    return (attended.astype(jnp.bfloat16), mixture)


def solution(mesh):
    placed = (
        P("ctx", "exp"),
        P("ctx", "exp"),
        P("ctx", "exp"),
        P("ctx", None),
        P("exp", None),
        P(),
        P(),
        P("ctx", None),
        P("exp", None, "ctx"),
        P("exp", None, "ctx"),
        P("exp", "ctx", None),
    )
    return jax.shard_map(
        local,
        mesh=mesh,
        in_specs=placed,
        out_specs=(P("ctx", None), P("ctx", "exp")),
        check_vma=False,
    )
```

profile of v0, /device:TPU:8, one launch (start us, length us, event | category | flops | bytes accessed | tf_op | source)
XLA Modules:
  0.0 393.7 jit_solution(3349251155809648889)
XLA Ops:
  7.2 1.5 pad_maximum_fusion
  8.7 0.0 all-reduce.4.cloned.1.call-start
  8.8 0.8 copy.56
  9.6 0.1 eq.50
  9.7 0.2 fusion.32
  9.9 51.7 %all-gather.4.cloned.1.call-done = bf16[2,2048,128]{2,1,0:T(8,128)(2,1)} async-done(((bf16[2,64,128]{2,1,0:T(8,128)(2,1)}), bf16[2,2048,128]{2,1,0:T(8,128)(2,1)}) %all-gather.4.cloned.1.call-update) | async-done | bytes 1048592 | tf_op jit(solution)/shard_map/all_gather | solution.py:35
  61.6 1.7 select_reduce_fusion
  63.3 0.5 fusion.8
  63.9 0.6 fusion.19
  64.4 1.1 copy-done.1
  65.5 1.7 convolution_convert_fusion.1
  67.3 0.1 fusion.38
  67.3 0.2 reduce_window_sum.11
  67.5 0.2 select_reduce_fusion.1
  67.7 72.7 %all-reduce.4.cloned.1.call-done = bf16[64,4096]{1,0:T(8,128)(2,1)} async-done(((bf16[64,4096]{1,0:T(8,128)(2,1)}), bf16[64,4096]{1,0:T(8,128)(2,1)}) %all-reduce.4.cloned.1.call-update) | async-done | bytes 524304 | tf_op jit(solution)/shard_map/psum | solution.py:65
  140.4 1.3 multiply_reduce_fusion
  141.8 2.1 multiply_convert_fusion
  143.8 2.0 broadcast_in_dim.62
  145.9 1.5 reshape.105
  147.4 0.9 fusion.1
  148.4 0.1 reshape.106
  148.5 0.1 copy.57
  148.6 0.1 reshape.124
  148.8 0.6 dynamic-slice.4
  150.0 0.2 fusion.40
  150.3 0.2 fusion.49
  150.5 1.0 gather_fusion
  151.5 0.1 reshape.127
  151.7 0.1 copy.58
  151.8 48.5 %all-gather.6.cloned.1.call-done = bf16[32,20,4096]{2,1,0:T(8,128)(2,1)} async-done(((bf16[1,20,4096]{2,1,0:T(8,128)(2,1)}), bf16[32,20,4096]{2,1,0:T(8,128)(2,1)}) %all-gather.6.cloned.1.call-update) | async-done | bytes 5242896 | tf_op jit(solution)/shard_map/all_gather | solution.py:87
  200.3 7.8 %reshape.138 = bf16[640,4096]{1,0:T(8,128)(2,1)} reshape(bf16[32,20,4096]{2,1,0:T(8,128)(2,1)} %all-gather.6.cloned.1.call-done) | data formatting | bytes 10485760
  208.1 4.9 %fusion.6 = f32[640,224]{0,1:T(8,128)S(1)} fusion(bf16[640,4096]{1,0:T(8,128)(2,1)} %reshape.138, bf16[1,4096,224]{1,2,0:T(8,128)(2,1)} %param.21), kind=kOutput, calls=%fused_computation.14 | convolution fusion | flops 1174405120 | bytes 7651328 | tf_op jit(solution)/shard_map/dot_general | solution.py:88
  213.0 9.7 %convolution_convert_fusion = bf16[640,4096]{1,0:T(8,128)(2,1)} fusion(bf16[1,224,4096]{2,1,0:T(8,128)(2,1)S(1)} %copy-done, bf16[640,4096]{1,0:T(8,128)(2,1)} %reshape.138, bf16[1,4096,224]{1,2,0:T(8,128)(2,1)} %param.22, f32[640,224]{0,1:T(8,128)S(1)} %fusion.6), kind=kOutput, calls=%fused_computation.3 | convolution fusion | flops 2352291840 | bytes 14729216 | tf_op jit(solution)/shard_map/dot_general | solution.py:92
  222.7 69.5 %fusion = bf16[24,4096]{1,0:T(8,128)(2,1)S(1)} fusion(bf16[640,4096]{1,0:T(8,128)(2,1)} %convolution_convert_fusion), kind=kCustom, calls=%all-reduce-scatter | all-reduce-scatter fusion | flops 3145729 | bytes 5440512
  292.3 1.9 collective-permute-start.5
  294.2 1.9 collective-permute-start.4
  296.2 4.2 %collective-permute-start.3 = (bf16[24,4096]{1,0:T(8,128)(2,1)S(1)}, bf16[24,4096]{1,0:T(8,128)(2,1)S(1)}, u32[]{:S(2)}, u32[]{:S(2)}) collective-permute-start(bf16[24,4096]{1,0:T(8,128)(2,1)S(1)} %fusion), channel_id=1, source_target_pairs={{0,32},{8,40},{16,48},{24,56},{32,64},{40,72},{48,80},{56,88},{64,... | collective-permute-start | bytes 589832
  300.4 1.9 collective-permute-start.2
  302.3 4.7 %collective-permute-start.1 = (bf16[24,4096]{1,0:T(8,128)(2,1)S(1)}, bf16[24,4096]{1,0:T(8,128)(2,1)S(1)}, u32[]{:S(2)}, u32[]{:S(2)}) collective-permute-start(bf16[24,4096]{1,0:T(8,128)(2,1)S(1)} %fusion), channel_id=1, source_target_pairs={{0,16},{8,24},{16,32},{24,40},{32,48},{40,56},{48,64},{56,72},{64,... | collective-permute-start | bytes 589832
  307.0 6.1 %collective-permute-start = (bf16[24,4096]{1,0:T(8,128)(2,1)S(1)}, bf16[24,4096]{1,0:T(8,128)(2,1)S(1)}, u32[]{:S(2)}, u32[]{:S(2)}) collective-permute-start(bf16[24,4096]{1,0:T(8,128)(2,1)S(1)} %fusion), channel_id=1, source_target_pairs={{0,8},{8,16},{16,24},{24,32},{32,40},{40,48},{48,56},{56,64},{64,7... | collective-permute-start | bytes 589832
  313.2 5.7 %collective-permute-done.1 = bf16[24,4096]{1,0:T(8,128)(2,1)S(1)} collective-permute-done((bf16[24,4096]{1,0:T(8,128)(2,1)S(1)}, bf16[24,4096]{1,0:T(8,128)(2,1)S(1)}, u32[]{:S(2)}, u32[]{:S(2)}) %collective-permute-start.1) | collective-permute-done | bytes 196640
  318.9 0.7 collective-permute-done
  319.7 17.7 %concatenate.3 = bf16[148,4096]{1,0:T(8,128)(2,1)} concatenate(bf16[4,4096]{1,0:T(4,128)(2,1)S(1)} %collective-permute-done.5, bf16[24,4096]{1,0:T(8,128)(2,1)S(1)} %collective-permute-done.4, bf16[24,4096]{1,0:T(8,128)(2,1)S(1)} %collective-permute-done.3, bf16[24,4096]{1,0:T(8,128)(2,1)S(1)} %collective-permute-done.2, bf16[24,4096]{1,0:T(8,128)(2,1)S(1)} %collective-permute-done.1, ...), dimensions={0} | concatenate | bytes 2424832
  337.4 1.0 dynamic-slice_convert_fusion
  338.4 0.9 gather_fusion.2
  339.3 1.8 gather_fusion.1
  341.2 2.3 fusion.22
  343.5 43.6 %reduce-scatter.4.cloned.1.call-done = bf16[64,512]{1,0:T(8,128)(2,1)} async-done(((bf16[64,4096]{1,0:T(8,128)(2,1)}), bf16[64,512]{1,0:T(8,128)(2,1)}) %reduce-scatter.4.cloned.1.call-update) | async-done | bytes 65552 | tf_op jit(solution)/shard_map/reduce_scatter | solution.py:105
  (39 shorter events, 0.3 us)
Async XLA Ops:
  7.2 205.9 %copy-start = (bf16[1,224,4096]{2,1,0:T(8,128)(2,1)S(1)}, bf16[1,224,4096]{2,1,0:T(8,128)(2,1)}, u32[]{:S(2)}) copy-start(bf16[1,224,4096]{2,1,0:T(8,128)(2,1)} %param.23) | copy-start | bytes 5505028
  7.2 54.4 %all-gather.4.cloned.1.call-start = ((), (), s32[]{:S(2)}) async-start(), calls=%async_computation.1 | async-start | bytes 1081344 | tf_op jit(solution)/shard_map/all_gather | solution.py:35
  8.7 131.7 %all-reduce.4.cloned.1.call-start = ((), (), s32[]{:S(2)}) async-start(), calls=%async_computation.2 | async-start | bytes 1048576 | tf_op jit(solution)/shard_map/psum | solution.py:65
  61.6 2.3 copy-start.7
  63.3 2.2 copy-start.1
  65.5 74.9 %copy-start.2 = (bf16[64,4096]{1,0:T(8,128)(2,1)S(1)}, bf16[64,4096]{1,0:T(8,128)(2,1)}, u32[]{:S(2)}) copy-start(bf16[64,4096]{1,0:T(8,128)(2,1)} %param.16) | copy-start | bytes 1572868
  65.5 76.2 %copy-start.4 = (f32[4096]{0:T(1024)S(1)}, f32[4096]{0:T(1024)}, u32[]{:S(2)}) copy-start(f32[4096]{0:T(1024)} %param.18) | copy-start | bytes 49156
  67.2 133.1 %all-gather.6.cloned.1.call-start = ((), (), s32[]{:S(2)}) async-start(), calls=%async_computation.4 | async-start | bytes 6488064 | tf_op jit(solution)/shard_map/all_gather | solution.py:87
  145.8 2.7 copy-start.5
  145.8 2.9 copy-start.6
  145.8 4.4 %copy-start.3 = (bf16[4096,8]{0,1:T(8,128)(2,1)S(1)}, bf16[4096,8]{0,1:T(8,128)(2,1)}, u32[]{:S(2)}) copy-start(bf16[4096,8]{0,1:T(8,128)(2,1)} %param.19) | copy-start | bytes 196612
  148.3 238.8 %reduce-scatter.4.cloned.1.call-start = ((), (), s32[]{:S(2)}) async-start(), calls=%async_computation.3 | async-start | bytes 589824 | tf_op jit(solution)/shard_map/reduce_scatter | solution.py:105
  292.3 14.7 %collective-permute-start.5 = (bf16[4,4096]{1,0:T(4,128)(2,1)S(1)}, bf16[4,4096]{1,0:T(4,128)(2,1)S(1)}, u32[]{:S(2)}, u32[]{:S(2)}) collective-permute-start(bf16[4,4096]{1,0:T(4,128)(2,1)S(1)} %slice.42), channel_id=1, source_target_pairs={{0,48},{8,56},{16,64},{24,72},{32,80},{40,88},{48,96},{56,104},{64... | collective-permute-start | bytes 98312
  294.2 18.9 %collective-permute-start.4 = (bf16[24,4096]{1,0:T(8,128)(2,1)S(1)}, bf16[24,4096]{1,0:T(8,128)(2,1)S(1)}, u32[]{:S(2)}, u32[]{:S(2)}) collective-permute-start(bf16[24,4096]{1,0:T(8,128)(2,1)S(1)} %fusion), channel_id=1, source_target_pairs={{0,40},{8,48},{16,56},{24,64},{32,72},{40,80},{48,88},{56,96},{64,... | collective-permute-start | bytes 589832
  296.2 17.0 %collective-permute-start.3 = (bf16[24,4096]{1,0:T(8,128)(2,1)S(1)}, bf16[24,4096]{1,0:T(8,128)(2,1)S(1)}, u32[]{:S(2)}, u32[]{:S(2)}) collective-permute-start(bf16[24,4096]{1,0:T(8,128)(2,1)S(1)} %fusion), channel_id=1, source_target_pairs={{0,32},{8,40},{16,48},{24,56},{32,64},{40,72},{48,80},{56,88},{64,... | collective-permute-start | bytes 589832
  300.4 12.8 %collective-permute-start.2 = (bf16[24,4096]{1,0:T(8,128)(2,1)S(1)}, bf16[24,4096]{1,0:T(8,128)(2,1)S(1)}, u32[]{:S(2)}, u32[]{:S(2)}) collective-permute-start(bf16[24,4096]{1,0:T(8,128)(2,1)S(1)} %fusion), channel_id=1, source_target_pairs={{0,24},{8,32},{16,40},{24,48},{32,56},{40,64},{48,72},{56,80},{64,... | collective-permute-start | bytes 589832
  302.3 16.6 %collective-permute-start.1 = (bf16[24,4096]{1,0:T(8,128)(2,1)S(1)}, bf16[24,4096]{1,0:T(8,128)(2,1)S(1)}, u32[]{:S(2)}, u32[]{:S(2)}) collective-permute-start(bf16[24,4096]{1,0:T(8,128)(2,1)S(1)} %fusion), channel_id=1, source_target_pairs={{0,16},{8,24},{16,32},{24,40},{32,48},{40,56},{48,64},{56,72},{64,... | collective-permute-start | bytes 589832
  307.0 12.7 %collective-permute-start = (bf16[24,4096]{1,0:T(8,128)(2,1)S(1)}, bf16[24,4096]{1,0:T(8,128)(2,1)S(1)}, u32[]{:S(2)}, u32[]{:S(2)}) collective-permute-start(bf16[24,4096]{1,0:T(8,128)(2,1)S(1)} %fusion), channel_id=1, source_target_pairs={{0,8},{8,16},{16,24},{24,32},{32,40},{40,48},{48,56},{56,64},{64,7... | collective-permute-start | bytes 589832
Sparse Core Ops, SparseCore 0:
  11.2 50.3 all-gather.3
  67.3 73.0 all-reduce.3
  148.4 51.7 all-gather.5
  343.6 43.4 reduce-scatter.3
where the time goes:
time: 396 us; the launch traced here: 394 us
  waiting for transfers between devices  223 us (56%)
  blocking collectives  69.5 us (18%)
  local copies, waits for them, and re-layouts  36 us (9%)
  starting transfers between devices  20.9 us (5%)
  matrix products  19.7 us (5%)
  between operations  14.8 us (4%)
  other arithmetic  9.59 us (2%)
    psum x1, waiting for transfers between devices, local(): lax.psum(projected.astype(jnp.bfloat16), 'exp').astype(jnp.float32)  72.7 us
    unnamed x1, blocking collectives  69.5 us
    all_gather x1, waiting for transfers between devices, local(): block_rows = lax.all_gather(key_value, 'ctx', axis=1, tiled=True)  51.7 us
    all_gather x1, waiting for transfers between devices, local(): block_rows = lax.all_gather(buffer, 'ctx', axis=0, tiled=True)  48.5 us
    reduce_scatter x1, waiting for transfers between devices, local(): lax.psum_scatter(contribution.astype(jnp.bfloat16), 'exp', scatter_dimens...  43.6 us
    unnamed x21, local copies, waits for them, and re-layouts  28 us
    unnamed x6, starting transfers between devices  20.8 us
    dot_general x1, matrix products, local(): jnp.dot(hidden, down_weight[0], preferred_element_type=jnp.float32)  9.68 us
  transfers between devices with their start and end apart: 10, of which 6 were waited for; matrix products, arithmetic and copies ran while one was open for 1% of the time, Pallas kernels for 0%

commit v1 on v0

v1 whole, which is shorter than its diff:
```python
import functools
import math

import jax
import jax.numpy as jnp
from jax import lax
from jax.experimental import pallas as pl
from jax.experimental.pallas import tpu as pltpu
from jax.sharding import PartitionSpec as P

WINDOW = 4096
SEQ = 2048
D = 4096
TOK = 64
CAP = 20
FF = 224
NZ = 8
COLS = D // NZ
HEAD = 128
GROUPS = 4
NB = 16
MAIN = 16
REM = CAP - MAIN
UNIT = COLS + 128
CUT = 384
BUNDLE = 4 * TOK
ROWS = NB * CAP
F32 = jnp.float32
BF16 = jnp.bfloat16
MESH = pl.DeviceIdType.MESH
HIGH = lax.Precision.HIGHEST
NT = (((1,), (1,)), ((), ()))

AG_LAGS = (1, 2, 3, 4)
RS_LAGS = (1, 2, 3, 4)


def iota(shape, dim):
    return lax.broadcasted_iota(jnp.int32, shape, dim)


def remote(src, dst, send, recv, device):
    return pltpu.make_async_remote_copy(
        src_ref=src, dst_ref=dst, send_sem=send, recv_sem=recv, device_id=device, device_id_type=MESH
    )


def wait(ref, sem):
    pltpu.make_async_copy(ref, ref, sem).wait()


def kernel(
    q_ref, k_ref, v_ref, res_ref, wo_ref, gain_ref, rt_ref, ids_ref, wg_ref, wu_ref, wd_ref,
    att_out, mix_out,
    qv, kv, qs, top, tot, acc, attn, wo, res, wg, wu, wd,
    sp, sm, rp, rm, att, ssum, lgt, place, perm, unperm,
    slots, scales, gate_acc, up_acc, hid, weight,
    part, r1p, r1m, r2p, r2m, r3p, r3m, r4p, r4m, yp, ym, tp, tm,
    ld, kvs, kvr, ws, wr, z1s, z1r, zas, zar, ags, agr, scs, scr, rss, rsr, z2s, z2r, outs,
):
    c = lax.axis_index("ctx")
    e = lax.axis_index("exp")
    core = lax.rem(c, 2)
    chip = lax.div(c, 2)
    x = lax.rem(chip, 4)
    y = lax.div(chip, 4)
    a = x + core * (y - x)
    b = y + core * (x - y)

    def ctx_of(aa, bb):
        return ((bb + core * (aa - bb)) * 4 + aa + core * (bb - aa)) * 2 + core

    ap, am, a2 = lax.rem(a + 1, 4), lax.rem(a + 3, 4), lax.rem(a + 2, 4)
    bp, bm, b2 = lax.rem(b + 1, 4), lax.rem(b + 3, 4), lax.rem(b + 2, 4)
    to_ap, to_am = (ctx_of(ap, b), e), (ctx_of(am, b), e)
    to_bp, to_bm = (ctx_of(a, bp), e), (ctx_of(a, bm), e)
    zp, zm = lax.rem(e + 1, NZ), lax.rem(e + NZ - 1, NZ)
    to_zp, to_zm = (c, zp), (c, zm)
    to_sib = (c + 1 - 2 * core, e)

    loads = [
        pltpu.make_async_copy(q_ref, qv, ld.at[0]),
        pltpu.make_async_copy(wo_ref, wo, ld.at[1]),
        pltpu.make_async_copy(
            res_ref.at[:, pl.ds(pl.multiple_of(e * COLS, COLS), COLS)], res, ld.at[2]
        ),
        pltpu.make_async_copy(wg_ref.at[0], wg.at[0:FF], ld.at[3]),
        pltpu.make_async_copy(wu_ref.at[0], wu.at[0:FF], ld.at[4]),
        pltpu.make_async_copy(wd_ref.at[0], wd.at[0:FF], ld.at[5]),
    ]

    def kv_rows(kk, bb, aa, units=1):
        return pl.ds(pl.multiple_of((kk * NB + bb * 4 + aa) * TOK, TOK), units * TOK)

    own = kv_rows(core, b, a)
    own_k = pltpu.make_async_copy(k_ref, kv.at[own, 0:HEAD], ld.at[6])
    own_v = pltpu.make_async_copy(v_ref, kv.at[own, HEAD : 2 * HEAD], ld.at[7])

    barrier = pltpu.get_barrier_semaphore()
    for other in (to_ap, to_am, to_bp, to_bm, to_zp, to_zm, to_sib):
        pl.semaphore_signal(barrier, inc=1, device_id=other, device_id_type=MESH)
    own_k.start()
    own_v.start()
    loads[0].start()
    pl.semaphore_wait(barrier, 7)

    k_own, v_own = kv.at[own, 0:HEAD], kv.at[own, HEAD : 2 * HEAD]
    kv_sent = []

    def kv_send(src, dst, i, device, recv=None):
        copy = remote(src, dst, kvs.at[len(kv_sent)], kvr.at[i], device)
        copy.start()
        kv_sent.append((dst, len(kv_sent)))

    kv_send(k_ref, k_own, 0, to_ap)
    kv_send(v_ref, v_own, 3, to_am)
    kv_send(v_ref, v_own, 1, to_ap)
    kv_send(k_ref, k_own, 2, to_am)
    for copy in loads[1:]:
        copy.start()
    w_sent = []
    for i, (src, dst) in enumerate(((wg_ref, wg), (wu_ref, wu), (wd_ref, wd))):
        copy = remote(src.at[0], dst.at[FF : 2 * FF], ws.at[i], wr.at[i], to_sib)
        copy.start()
        w_sent.append((dst.at[FF : 2 * FF], i))

    ids = ids_ref[...]
    first_id, second_id = ids[0:1, :], ids[1:2, :]
    mine = jnp.where((first_id == e) | (second_id == e), 1.0, 0.0)
    before = jnp.where(iota((TOK, TOK), 0) < iota((TOK, TOK), 1), 1.0, 0.0).astype(BF16)
    slot = jnp.dot(
        jnp.broadcast_to(mine, (8, TOK)).astype(BF16), before, preferred_element_type=F32
    )[0:1, :]
    slot = jnp.where(mine > 0.0, slot, -1.0)
    row = iota((2 * MAIN, TOK), 0)
    wanted = jnp.where(row < MAIN, row, MAIN + lax.rem(row, REM)).astype(F32)
    place[...] = jnp.where(jnp.broadcast_to(slot, (2 * MAIN, TOK)) == wanted, 1.0, 0.0).astype(BF16)
    by_token = jnp.where(
        jnp.broadcast_to(slot, (HEAD, TOK)) == iota((HEAD, TOK), 0).astype(F32), 1.0, 0.0
    ).astype(BF16)
    eye = jnp.where(iota((TOK, TOK), 0) == iota((TOK, TOK), 1), 1.0, 0.0)
    slot_of_token = lax.dot_general(eye.astype(BF16), by_token, NT, preferred_element_type=F32)

    r256, l256 = iota((256, 256), 0), iota((256, 256), 1)
    i64 = lax.rem(r256, 64)
    to_unit = lax.div(i64, REM) * 16 + lax.div(r256, 64) * REM + lax.rem(i64, REM)
    perm[...] = jnp.where(l256 == to_unit, 1.0, 0.0).astype(BF16)
    to_flat = lax.rem(lax.div(r256, REM), 4) * 64 + lax.div(r256, 16) * REM + lax.rem(r256, REM)
    unperm[...] = jnp.where(l256 == to_flat, 1.0, 0.0).astype(BF16)

    gate_acc[...] = jnp.zeros_like(gate_acc)
    up_acc[...] = jnp.zeros_like(up_acc)
    ssum[...] = jnp.zeros_like(ssum)
    lgt[...] = jnp.zeros_like(lgt)
    half = COLS // 2
    tp[0, :, half:] = jnp.zeros((TOK, half), BF16)
    tm[0, :, :half] = jnp.zeros((TOK, half), BF16)
    top[...] = jnp.full(top.shape, -1e30, F32)
    tot[...] = jnp.zeros_like(tot)
    acc[...] = jnp.zeros_like(acc)

    loads[0].wait()
    for g in range(GROUPS):
        qs[g * TOK : (g + 1) * TOK, :] = qv[:, g * HEAD : (g + 1) * HEAD]

    rows_m, rows_p, rows_2 = kv_rows(core, b, am), kv_rows(core, b, ap), kv_rows(core, b, a2)
    klane, vlane = slice(0, HEAD), slice(HEAD, 2 * HEAD)
    wait(kv.at[rows_m, klane], kvr.at[0])
    kv_send(kv.at[rows_m, klane], kv.at[rows_m, klane], 4, to_ap)
    wait(kv.at[rows_p, vlane], kvr.at[3])
    kv_send(kv.at[rows_p, vlane], kv.at[rows_p, vlane], 5, to_am)
    wait(kv.at[rows_m, vlane], kvr.at[1])
    wait(kv.at[rows_p, klane], kvr.at[2])
    own_k.wait()
    own_v.wait()
    wait(kv.at[rows_2, klane], kvr.at[4])
    wait(kv.at[rows_2, vlane], kvr.at[5])
    whole = kv_rows(core, b, 0, 4)
    kv_send(kv.at[whole, :], kv.at[whole, :], 6, to_bp)
    kv_send(kv.at[whole, :], kv.at[whole, :], 7, to_bm)
    kv_send(kv.at[whole, :], kv.at[whole, :], 10, to_sib)

    query_pos = c * TOK + lax.rem(iota((GROUPS * TOK, 1), 0), TOK)
    lane = iota((1, BUNDLE), 1)
    score_scale = 1.0 / math.sqrt(HEAD)

    def attend(kk, bb):
        rows = kv_rows(kk, bb, 0, 4)
        key_pos = (
            TOK * kk
            + lax.rem(lane, TOK)
            + 2 * TOK * ((1 + 3 * kk) * lax.div(lane, TOK) + (4 - 3 * kk) * bb)
        )
        scores = (
            lax.dot_general(qs[...], kv[rows, klane], NT, preferred_element_type=F32) * score_scale
        )
        allowed = key_pos <= query_pos
        if SEQ > WINDOW:
            allowed = allowed & (key_pos > query_pos - WINDOW)
        scores = jnp.where(allowed, scores, -1e30)
        old = top[:, 0:1]
        new = jnp.maximum(old, jnp.max(scores, axis=1, keepdims=True))
        fade = jnp.exp(old - new)
        weights = jnp.exp(scores - new)
        top[...] = jnp.broadcast_to(new, top.shape)
        tot[...] = tot[...] * fade + jnp.sum(weights, axis=1, keepdims=True)
        acc[...] = acc[...] * fade + jnp.dot(
            weights.astype(BF16), kv[rows, vlane], preferred_element_type=F32
        )

    def other_wait(aa, i):
        wait(kv.at[kv_rows(1 - core, aa, 0, 4), :], kvr.at[i])

    def halves(bb):
        first = pl.multiple_of((core * NB + bb * 4) * TOK, TOK)
        return pl.ds(first, 2 * TOK), pl.ds(pl.multiple_of(first + 2 * TOK, TOK), 2 * TOK)

    attend(core, b)
    other_wait(a, 10)
    attend(1 - core, a)
    whole_m, whole_p, whole_2 = (kv_rows(core, bb, 0, 4) for bb in (bm, bp, b2))
    wait(kv.at[whole_m, :], kvr.at[6])
    kv_send(kv.at[halves(bm)[0], :], kv.at[halves(bm)[0], :], 8, to_bp)
    kv_send(kv.at[whole_m, :], kv.at[whole_m, :], 11, to_sib)
    wait(kv.at[whole_p, :], kvr.at[7])
    kv_send(kv.at[halves(bp)[1], :], kv.at[halves(bp)[1], :], 9, to_bm)
    kv_send(kv.at[whole_p, :], kv.at[whole_p, :], 12, to_sib)
    attend(core, bm)
    attend(core, bp)
    wait(kv.at[halves(b2)[0], :], kvr.at[8])
    wait(kv.at[halves(b2)[1], :], kvr.at[9])
    kv_send(kv.at[whole_2, :], kv.at[whole_2, :], 13, to_sib)
    other_wait(am, 11)
    attend(1 - core, am)
    other_wait(ap, 12)
    attend(1 - core, ap)
    attend(core, b2)
    other_wait(a2, 13)
    attend(1 - core, a2)

    for g in range(GROUPS):
        rows = slice(g * TOK, (g + 1) * TOK)
        attn[:, g * HEAD : (g + 1) * HEAD] = (acc[rows, :] / tot[rows, 0:1]).astype(BF16)

    def chunk(s):
        return lax.rem(e + s + NZ, NZ)

    def cols(j):
        return pl.ds(pl.multiple_of(j * COLS, COLS), COLS)

    def project(s):
        return jnp.dot(attn[...], wo[:, cols(chunk(s))], preferred_element_type=F32)

    lo, hi = slice(0, half), slice(half, COLS)
    loads[1].wait()
    far = project(4).astype(BF16)
    sp[0] = far
    remote(sp.at[0, :, lo], rp.at[0, :, lo], z1s.at[0], z1r.at[0], to_zp).start()
    remote(sp.at[0, :, hi], rm.at[0, :, hi], z1s.at[4], z1r.at[4], to_zm).start()
    for i in range(1, 4):
        up, down = project(4 - i), project(i - 4)
        if i == 1:
            wait(rp.at[0, :, lo], z1r.at[0])
            sp[1, :, lo] = (up[:, lo] + rp[0, :, lo].astype(F32)).astype(BF16)
            sp[1, :, hi] = up[:, hi].astype(BF16)
        else:
            wait(rp.at[i - 1], z1r.at[i - 1])
            sp[i] = (up + rp[i - 1].astype(F32)).astype(BF16)
        remote(sp.at[i], rp.at[i], z1s.at[i], z1r.at[i], to_zp).start()
        if i == 1:
            wait(rm.at[0, :, hi], z1r.at[4])
            sm[1, :, hi] = (down[:, hi] + rm[0, :, hi].astype(F32)).astype(BF16)
            sm[1, :, lo] = down[:, lo].astype(BF16)
        else:
            wait(rm.at[i - 1], z1r.at[4 + i - 1])
            sm[i] = (down + rm[i - 1].astype(F32)).astype(BF16)
        remote(sm.at[i], rm.at[i], z1s.at[4 + i], z1r.at[4 + i], to_zm).start()
    loads[2].wait()
    total = project(0) + res[...].astype(F32)
    wait(rp.at[3], z1r.at[3])
    wait(rm.at[3], z1r.at[7])
    att[e] = (total + rp[3].astype(F32) + rm[3].astype(F32)).astype(BF16)
    remote(att.at[e], att.at[e], zas.at[0], zar.at[2], to_zp).start()
    remote(att.at[e], att.at[e], zas.at[7], zar.at[1], to_zm).start()

    def ag_chunk(n):
        odd = lax.rem(n, 2)
        return chunk((2 * odd - 1) * lax.div(n + 1, 2))

    def unit(aa, bb):
        return pl.ds(pl.multiple_of((bb * 4 + aa) * MAIN, MAIN), MAIN)

    def bundle(bb):
        return pl.ds(pl.multiple_of(bb * 64, 64), 64)

    def first_half(bb):
        return pl.ds(pl.multiple_of(bb * 64, 32), 32)

    def second_half(bb):
        return pl.ds(pl.multiple_of(bb * 64 + 32, 32), 32)

    def scale_unit(aa, bb):
        return pl.ds(pl.multiple_of((bb * 4 + aa) * 8, 8), 8)

    def scale_bundle(bb):
        return pl.ds(pl.multiple_of(bb * 32, 8), 32)

    def out_copy(j):
        return pltpu.make_async_copy(att.at[j], att_out.at[:, cols(j)], outs.at[j])

    def left(rows, cut):
        return rows, slice(0, cut)

    def ag_start(n):
        j = ag_chunk(n)
        odd = lax.rem(n, 2)

        @pl.when((n > 0) & (n < 7))
        def _():
            wait(att.at[j], zar.at[n])

        @pl.when((n > 0) & (n < 5))
        def _():
            remote(
                att.at[j], att.at[j], zas.at[n], zar.at[n + 2], (c, lax.rem(e + 1 - 2 * odd + NZ, NZ))
            ).start()

        @pl.when(n == 5)
        def _():
            remote(att.at[j, :, hi], att.at[j, :, hi], zas.at[5], zar.at[8], to_zm).start()

        @pl.when(n == 6)
        def _():
            remote(att.at[j, :, lo], att.at[j, :, lo], zas.at[6], zar.at[7], to_zp).start()

        @pl.when(n == 7)
        def _():
            wait(att.at[j, :, lo], zar.at[7])
            wait(att.at[j, :, hi], zar.at[8])

        out_copy(j).start()
        value = att[j].astype(F32)
        scaled = (value * gain_ref[:, cols(j)]).astype(BF16)
        packed = jnp.dot(place[...], scaled, preferred_element_type=F32)
        mine_rows = unit(a, b)
        slots[j, mine_rows, 0:COLS] = packed[0:MAIN].astype(BF16)
        tile = lax.div(iota((MAIN, 128), 0), REM)
        rest = jnp.zeros((MAIN, 128), F32)
        for t in range(4):
            rest = rest + jnp.where(tile == t, packed[MAIN:, t * 128 : (t + 1) * 128], 0.0)
        slots[j, mine_rows, COLS:UNIT] = rest.astype(BF16)
        here = slots.at[j, mine_rows, :]
        remote(here, here, ags.at[0, n], agr.at[0, n], to_ap).start()
        remote(here, here, ags.at[1, n], agr.at[1, n], to_am).start()
        ssum[...] += jnp.sum(value * value, axis=1, keepdims=True)
        lgt[...] += lax.dot_general(rt_ref[:, cols(j)], scaled, NT, preferred_element_type=F32)

        @pl.when(n == 7)
        def _():
            inverse = lax.rsqrt(ssum[:, 0:1] * (1.0 / D) + 1e-05)
            by_slot = jnp.sum(slot_of_token * inverse, axis=0, keepdims=True)
            scales[scale_unit(a, b), :] = jnp.broadcast_to(by_slot, (8, HEAD))
            here = scales.at[scale_unit(a, b), :]
            remote(here, here, scs.at[0], scr.at[0], to_ap).start()
            remote(here, here, scs.at[1], scr.at[1], to_am).start()
            inverse_row = jnp.sum(eye * inverse, axis=0, keepdims=True)
            logits = lgt[...] * inverse_row
            number = iota((NZ, TOK), 0)
            one = jnp.sum(jnp.where(number == first_id, logits, 0.0), axis=0, keepdims=True)
            two = jnp.sum(jnp.where(number == second_id, logits, 0.0), axis=0, keepdims=True)
            gate = 1.0 / (1.0 + jnp.exp(two - one))
            gate = jnp.where(first_id == e, gate, 1.0 - gate)
            spread = jnp.where(
                jnp.broadcast_to(slot, (2 * MAIN, TOK)) == wanted,
                jnp.broadcast_to(gate, (2 * MAIN, TOK)),
                0.0,
            )
            weight[...] = lax.dot_general(
                eye, spread, NT, precision=HIGH, preferred_element_type=F32
            )

    def ag_first(n):
        j = ag_chunk(n)
        at_m, at_p = unit(am, b), unit(ap, b)
        wait(slots.at[j, at_m, :], agr.at[0, n])
        piece = slots.at[j, at_m, 0:CUT]
        remote(piece, piece, ags.at[2, n], agr.at[2, n], to_ap).start()
        wait(slots.at[j, at_p, :], agr.at[1, n])
        piece = slots.at[j, at_p, CUT:UNIT]
        remote(piece, piece, ags.at[3, n], agr.at[3, n], to_am).start()

        @pl.when(n == 7)
        def _():
            piece = scales.at[scale_unit(am, b), :]
            wait(piece, scr.at[0])
            remote(piece, piece, scs.at[2], scr.at[2], to_ap).start()
            wait(scales.at[scale_unit(ap, b), :], scr.at[1])

    def ag_second(n):
        j = ag_chunk(n)
        at_2 = unit(a2, b)
        wait(slots.at[j, at_2, 0:CUT], agr.at[2, n])
        wait(slots.at[j, at_2, CUT:UNIT], agr.at[3, n])
        piece = slots.at[j, bundle(b), :]
        remote(piece, piece, ags.at[4, n], agr.at[4, n], to_bp).start()
        remote(piece, piece, ags.at[5, n], agr.at[5, n], to_bm).start()

        @pl.when(n == 7)
        def _():
            wait(scales.at[scale_unit(a2, b), :], scr.at[2])
            piece = scales.at[scale_bundle(b), :]
            remote(piece, piece, scs.at[3], scr.at[3], to_bp).start()
            remote(piece, piece, scs.at[4], scr.at[4], to_bm).start()

    def ag_third(n):
        j = ag_chunk(n)
        wait(slots.at[j, bundle(bm), :], agr.at[4, n])
        piece = slots.at[j, first_half(bm), :]
        remote(piece, piece, ags.at[6, n], agr.at[6, n], to_bp).start()
        wait(slots.at[j, bundle(bp), :], agr.at[5, n])
        piece = slots.at[j, second_half(bp), :]
        remote(piece, piece, ags.at[7, n], agr.at[7, n], to_bm).start()

        @pl.when(n == 7)
        def _():
            piece = scales.at[scale_bundle(bm), :]
            wait(piece, scr.at[3])
            remote(piece, piece, scs.at[5], scr.at[5], to_bp).start()
            wait(scales.at[scale_bundle(bp), :], scr.at[4])

    def ag_use(n):
        j = ag_chunk(n)
        wait(slots.at[j, first_half(b2), :], agr.at[6, n])
        wait(slots.at[j, second_half(b2), :], agr.at[7, n])
        flat = jnp.dot(
            perm[...], slots[j, 0:256, COLS:UNIT], preferred_element_type=F32
        ).astype(BF16)
        for t in range(4):
            slots[j, 256:ROWS, t * 128 : (t + 1) * 128] = flat[t * 64 : (t + 1) * 64]
        rows = slots[j, :, 0:COLS]
        gate_acc[...] += lax.dot_general(rows, wg[:, cols(j)], NT, preferred_element_type=F32)
        up_acc[...] += lax.dot_general(rows, wu[:, cols(j)], NT, preferred_element_type=F32)

    def run(stages, count):
        last = max(lag for _, lag in stages)

        def tick(t, carry):
            for function, lag in stages:

                @pl.when((t >= lag) & (t < lag + count))
                def _(function=function, lag=lag):
                    function(t - lag)

            return carry

        lax.fori_loop(0, count + last, tick, 0)

    loads[3].wait()
    loads[4].wait()
    wait(wg.at[FF : 2 * FF], wr.at[0])
    wait(wu.at[FF : 2 * FF], wr.at[1])
    run(
        (
            (ag_third, AG_LAGS[2]),
            (ag_second, AG_LAGS[1]),
            (ag_first, AG_LAGS[0]),
            (ag_start, 0),
            (ag_use, AG_LAGS[3]),
        ),
        NZ,
    )
    wait(scales.at[scale_bundle(b2), :], scr.at[5])

    row = iota((ROWS, HEAD), 0)
    col = iota((ROWS, HEAD), 1)
    over = row - 256
    block_of = jnp.where(row < 256, lax.div(row, MAIN), lax.div(over, REM))
    slot_of = jnp.where(row < 256, lax.rem(row, MAIN), MAIN + lax.rem(over + 256, REM))
    pick = jnp.where(col == block_of * 8, 1.0, 0.0)
    spread = jnp.dot(pick, scales[...], precision=HIGH, preferred_element_type=F32)
    factor = jnp.sum(jnp.where(col == slot_of, spread, 0.0), axis=1, keepdims=True)
    gated = gate_acc[...] * factor
    hid[...] = (gated / (1.0 + jnp.exp(-gated)) * (up_acc[...] * factor)).astype(BF16)
    loads[5].wait()
    wait(wd.at[FF : 2 * FF], wr.at[2])

    def rs_chunk(n):
        odd = lax.rem(n, 2)
        return chunk(odd * (4 - lax.div(n + 1, 2)) - (1 - odd) * (4 - lax.div(n, 2)))

    def rs_start(n):
        j = rs_chunk(n)
        out = jnp.dot(hid[...], wd[:, cols(j)], preferred_element_type=F32).astype(BF16)
        part[n, :, 0:COLS] = out[0:256]
        rest = jnp.concatenate([out[256:, t * 128 : (t + 1) * 128] for t in range(4)], axis=0)
        part[n, :, COLS:UNIT] = jnp.dot(unperm[...], rest, preferred_element_type=F32).astype(BF16)
        remote(
            part.at[n, first_half(b2), :], r1p.at[n], rss.at[0, n], rsr.at[0, n], to_bp
        ).start()
        remote(
            part.at[n, second_half(b2), :], r1m.at[n], rss.at[1, n], rsr.at[1, n], to_bm
        ).start()

    def add(n, rows, lanes, more):
        value = part[n, rows, lanes].astype(F32)
        for term in more:
            value = value + term.astype(F32)
        return value

    every = slice(0, UNIT)

    def rs_first(n):
        wait(r1p.at[n], rsr.at[0, n])
        rows = first_half(bp)
        part[n, rows, every] = add(n, rows, every, [r1p[n]]).astype(BF16)
        remote(part.at[n, bundle(bp), :], r2p.at[n], rss.at[2, n], rsr.at[2, n], to_bp).start()
        wait(r1m.at[n], rsr.at[1, n])
        rows = second_half(bm)
        part[n, rows, every] = add(n, rows, every, [r1m[n]]).astype(BF16)
        remote(part.at[n, bundle(bm), :], r2m.at[n], rss.at[3, n], rsr.at[3, n], to_bm).start()

    def rs_second(n):
        wait(r2p.at[n], rsr.at[2, n])
        wait(r2m.at[n], rsr.at[3, n])
        rows = bundle(b)
        part[n, rows, every] = add(n, rows, every, [r2p[n], r2m[n]]).astype(BF16)
        at_2 = unit(a2, b)
        remote(
            part.at[n, at_2, 0:CUT], r3p.at[n], rss.at[4, n], rsr.at[4, n], to_ap
        ).start()
        remote(
            part.at[n, at_2, CUT:UNIT], r3m.at[n], rss.at[5, n], rsr.at[5, n], to_am
        ).start()

    def rs_third(n):
        at_p, at_m = unit(ap, b), unit(am, b)
        wait(r3p.at[n], rsr.at[4, n])
        part[n, at_p, 0:CUT] = add(n, at_p, slice(0, CUT), [r3p[n]]).astype(BF16)
        remote(part.at[n, at_p, :], r4p.at[n], rss.at[6, n], rsr.at[6, n], to_ap).start()
        wait(r3m.at[n], rsr.at[5, n])
        part[n, at_m, CUT:UNIT] = add(n, at_m, slice(CUT, UNIT), [r3m[n]]).astype(BF16)
        remote(part.at[n, at_m, :], r4m.at[n], rss.at[7, n], rsr.at[7, n], to_am).start()

    def rs_last(n):
        wait(r4p.at[n], rsr.at[6, n])
        wait(r4m.at[n], rsr.at[7, n])
        mine_sum = add(n, unit(a, b), every, [r4p[n], r4m[n]])
        tile = lax.div(iota((MAIN, 128), 0), REM)
        rest = jnp.concatenate(
            [jnp.where(tile == t, mine_sum[:, COLS:UNIT], 0.0) for t in range(4)], axis=1
        )
        terms = jnp.concatenate([mine_sum[:, 0:COLS], rest], axis=0)
        mixed = jnp.dot(weight[...], terms, precision=HIGH, preferred_element_type=F32)
        odd = lax.rem(n, 2)
        i = lax.div(n + 1, 2)

        @pl.when(n == 0)
        def _():
            yp[0] = mixed.astype(BF16)
            remote(yp.at[0, :, lo], tp.at[0, :, lo], z2s.at[0], z2r.at[0], to_zp).start()
            remote(yp.at[0, :, hi], tm.at[0, :, hi], z2s.at[4], z2r.at[4], to_zm).start()

        @pl.when(n == 1)
        def _():
            wait(tp.at[0, :, lo], z2r.at[0])

        @pl.when(n == 2)
        def _():
            wait(tm.at[0, :, hi], z2r.at[4])

        @pl.when((n > 2) & (odd == 1))
        def _():
            wait(tp.at[i - 1], z2r.at[i - 1])

        @pl.when((n > 2) & (odd == 0))
        def _():
            wait(tm.at[i - 1], z2r.at[4 + i - 1])

        @pl.when((n < 7) & (odd == 1))
        def _():
            yp[i] = (mixed + tp[i - 1].astype(F32)).astype(BF16)
            remote(yp.at[i], tp.at[i], z2s.at[i], z2r.at[i], to_zp).start()

        @pl.when((n > 0) & (odd == 0))
        def _():
            ym[i] = (mixed + tm[i - 1].astype(F32)).astype(BF16)
            remote(ym.at[i], tm.at[i], z2s.at[4 + i], z2r.at[4 + i], to_zm).start()

        @pl.when(n == 7)
        def _():
            wait(tm.at[3], z2r.at[7])
            mix_out[...] = (mixed + tp[3].astype(F32) + tm[3].astype(F32)).astype(BF16)

    run(
        (
            (rs_last, RS_LAGS[3]),
            (rs_third, RS_LAGS[2]),
            (rs_second, RS_LAGS[1]),
            (rs_first, RS_LAGS[0]),
            (rs_start, 0),
        ),
        NZ,
    )

    for ref, i in kv_sent:
        wait(ref, kvs.at[i])
    for ref, i in w_sent:
        wait(ref, ws.at[i])
    for i in range(8):
        part_of = (slice(None), lo) if i == 0 else (slice(None), hi) if i == 4 else (slice(None),) * 2
        wait(sp.at[(0,) + part_of], z1s.at[i])
        wait(yp.at[(0,) + part_of], z2s.at[i])

    def drain(n, carry):
        for i, piece in enumerate(
            (
                slots.at[0, 0:MAIN, :], slots.at[0, 0:MAIN, :], slots.at[0, 0:MAIN, 0:CUT],
                slots.at[0, 0:MAIN, CUT:UNIT], slots.at[0, 0:64, :], slots.at[0, 0:64, :],
                slots.at[0, 0:32, :], slots.at[0, 0:32, :],
            )
        ):
            wait(piece, ags.at[i, n])
        for i, piece in enumerate((r1p, r1m, r2p, r2m, r3p, r3m, r4p, r4m)):
            wait(piece.at[0], rss.at[i, n])
        out_copy(n).wait()
        return carry

    lax.fori_loop(0, NZ, drain, 0)
    for i in range(8):
        piece = att.at[0, :, hi] if i == 5 else att.at[0, :, lo] if i == 6 else att.at[0]
        wait(piece, zas.at[i])
    for i in range(6):
        wait(scales.at[0:8, :] if i < 3 else scales.at[0:32, :], scs.at[i])


def local(
    query, key_states, value_states, residual, out_weight, norm_gain, router_weight, expert_ids,
    gate_weight, up_weight, down_weight,
):
    anywhere = pl.BlockSpec(memory_space=pl.ANY)
    near = pl.BlockSpec(memory_space=pltpu.VMEM)
    vmem = pltpu.VMEM
    dma = pltpu.SemaphoreType.DMA
    scratch = [
        vmem((TOK, GROUPS * HEAD), BF16),
        vmem((SEQ, 2 * HEAD), BF16),
        vmem((GROUPS * TOK, HEAD), BF16),
        vmem((GROUPS * TOK, HEAD), F32),
        vmem((GROUPS * TOK, HEAD), F32),
        vmem((GROUPS * TOK, HEAD), F32),
        vmem((TOK, GROUPS * HEAD), BF16),
        vmem((GROUPS * HEAD, D), BF16),
        vmem((TOK, COLS), BF16),
        vmem((2 * FF, D), BF16),
        vmem((2 * FF, D), BF16),
        vmem((2 * FF, D), BF16),
        vmem((4, TOK, COLS), BF16),
        vmem((4, TOK, COLS), BF16),
        vmem((4, TOK, COLS), BF16),
        vmem((4, TOK, COLS), BF16),
        vmem((NZ, TOK, COLS), BF16),
        vmem((TOK, HEAD), F32),
        vmem((NZ, TOK), F32),
        vmem((2 * MAIN, TOK), BF16),
        vmem((256, 256), BF16),
        vmem((256, 256), BF16),
        vmem((NZ, ROWS, UNIT), BF16),
        vmem((NB * 8, HEAD), F32),
        vmem((ROWS, 2 * FF), F32),
        vmem((ROWS, 2 * FF), F32),
        vmem((ROWS, 2 * FF), BF16),
        vmem((TOK, 2 * MAIN), F32),
        vmem((NZ, 256, UNIT), BF16),
        vmem((NZ, 32, UNIT), BF16),
        vmem((NZ, 32, UNIT), BF16),
        vmem((NZ, 64, UNIT), BF16),
        vmem((NZ, 64, UNIT), BF16),
        vmem((NZ, MAIN, CUT), BF16),
        vmem((NZ, MAIN, UNIT - CUT), BF16),
        vmem((NZ, MAIN, UNIT), BF16),
        vmem((NZ, MAIN, UNIT), BF16),
        vmem((4, TOK, COLS), BF16),
        vmem((4, TOK, COLS), BF16),
        vmem((4, TOK, COLS), BF16),
        vmem((4, TOK, COLS), BF16),
        dma((8,)),
        dma((14,)),
        dma((14,)),
        dma((3,)),
        dma((3,)),
        dma((8,)),
        dma((8,)),
        dma((8,)),
        dma((9,)),
        dma((8, NZ)),
        dma((8, NZ)),
        dma((6,)),
        dma((6,)),
        dma((8, NZ)),
        dma((8, NZ)),
        dma((8,)),
        dma((8,)),
        dma((NZ,)),
    ]
    return pl.pallas_call(
        kernel,
        out_shape=(
            jax.ShapeDtypeStruct((TOK, D), BF16),
            jax.ShapeDtypeStruct((TOK, COLS), BF16),
        ),
        in_specs=[anywhere] * 5 + [near] * 3 + [anywhere] * 3,
        out_specs=(anywhere, near),
        scratch_shapes=scratch,
        compiler_params=pltpu.CompilerParams(
            collective_id=0, has_side_effects=True, vmem_limit_bytes=56 * 1024 * 1024
        ),
        name="layer",
    )(
        query,
        key_states,
        value_states,
        residual,
        out_weight,
        norm_gain.reshape(1, D),
        router_weight.T,
        expert_ids.T,
        jnp.swapaxes(gate_weight, 1, 2),
        jnp.swapaxes(up_weight, 1, 2),
        down_weight,
    )


def solution(mesh):
    placed = (
        P("ctx", "exp"),
        P("ctx", "exp"),
        P("ctx", "exp"),
        P("ctx", None),
        P("exp", None),
        P(),
        P(),
        P("ctx", None),
        P("exp", None, "ctx"),
        P("exp", None, "ctx"),
        P("exp", "ctx", None),
    )
    return jax.shard_map(
        local,
        mesh=mesh,
        in_specs=placed,
        out_specs=(P("ctx", None), P("ctx", "exp")),
        check_vma=False,
    )
```

time: 396 us -> 140 us (0.35)
  waiting for transfers between devices: 223 us -> 0 us
  Pallas kernels: 0 us -> 135 us
  blocking collectives: 69.5 us -> 0 us
  local copies, waits for them, and re-layouts: 36 us -> 3.34 us
  starting transfers between devices: 20.9 us -> 0 us
  matrix products: 19.7 us -> 0 us
  between operations: 14.8 us -> 0.64 us
  other arithmetic: 9.59 us -> 0 us
    pallas_call x0 -> x1, Pallas kernels: none -> 135 us  [local(): pl.pallas_call(kernel, out_shape=(jax.ShapeDtypeStruct((TOK, D), BF16), j...]
    all_gather x2 -> x0, waiting for transfers between devices: 100 us -> none  [the longest x1 51.7 us: local(): block_rows = lax.all_gather(key_value, 'ctx', axis=1, tiled=True)]
    psum x1 -> x0, waiting for transfers between devices: 72.7 us -> none  [local(): lax.psum(projected.astype(jnp.bfloat16), 'exp').astype(jnp.float32)]
    unnamed x1 -> x0, blocking collectives: 69.5 us -> none
    reduce_scatter x1 -> x0, waiting for transfers between devices: 43.6 us -> none  [local(): lax.psum_scatter(contribution.astype(jnp.bfloat16), 'exp', scatter_dimens...]
    unnamed x21 -> x2, local copies, waits for them, and re-layouts: 28 us -> 3.34 us
    unnamed x6 -> x0, starting transfers between devices: 20.8 us -> none
    dot_general x7 -> x0, matrix products: 19.7 us -> none  [the longest x1 9.68 us: local(): jnp.dot(hidden, down_weight[0], preferred_element_type=jnp.float32)]
  transfers between devices with their start and end apart: 10 -> 0, of which waited for: 6 -> 0; matrix products, arithmetic and copies ran while one was open for 1% -> 0% of each run, Pallas kernels for 0% -> 0%
where the time goes in v1:
time: 140 us; the launch traced here: 139 us
  Pallas kernels  135 us (96%)
  local copies, waits for them, and re-layouts  3.34 us (2%)
    pallas_call x1, Pallas kernels, local(): pl.pallas_call(kernel, out_shape=(jax.ShapeDtypeStruct((TOK, D), BF16), j...  135 us
    unnamed x2, local copies, waits for them, and re-layouts  3.34 us

profile of v1, /device:TPU:8, one launch (start us, length us, event | category | flops | bytes accessed | tf_op | source)
XLA Modules:
  0.0 139.4 jit_solution(3307384550400555868)
XLA Ops:
  0.6 135.4 %layer.1 = (bf16[64,4096]{1,0:T(8,128)(2,1)}, bf16[64,512]{1,0:T(8,128)(2,1)}) custom-call(bf16[64,512]{1,0:T(8,128)(2,1)} %q_ref.1, bf16[64,128]{1,0:T(8,128)(2,1)} %k_ref.1, bf16[64,128]{1,0:T(8,128)(2,1)} %v_ref.1, bf16[64,4096]{1,0:T(8,128)(2,1)} %res_ref.1, bf16[512,4096]{1,0:T(8,128)(2,1)} %wo_ref.1, f32[1,4096]{1,0:T(1,128)} %bitcast.8, ...), custom_call_target="tpu_custom_call" | custom-call | tf_op jit(solution)/shard_map/layer/pallas_call | solution.py:705
  136.0 1.9 %copy.15 = bf16[64,4096]{1,0:T(8,128)(2,1)} copy(bf16[64,4096]{1,0:T(8,128)(2,1)} %get-tuple-element.4) | data formatting | bytes 1048576
  137.9 1.5 %copy.16 = bf16[64,512]{1,0:T(8,128)(2,1)} copy(bf16[64,512]{1,0:T(8,128)(2,1)} %get-tuple-element.5) | data formatting | bytes 131072

commit v2 on v1

v2 whole, which is shorter than its diff:
```python
import functools
import math

import jax
import jax.numpy as jnp
from jax import lax
from jax.experimental import pallas as pl
from jax.experimental.pallas import tpu as pltpu
from jax.sharding import PartitionSpec as P

WINDOW = 4096
SEQ = 2048
D = 4096
TOK = 64
CAP = 20
FF = 224
NZ = 8
COLS = D // NZ
HEAD = 128
GROUPS = 4
NB = 16
MAIN = 16
REM = CAP - MAIN
UNIT = COLS + 128
BUNDLE = 4 * TOK
ROWS = NB * CAP
F32 = jnp.float32
BF16 = jnp.bfloat16
MESH = pl.DeviceIdType.MESH
HIGH = lax.Precision.HIGHEST
NT = (((1,), (1,)), ((), ()))

AG_LAGS = (3, 6, 9)
RS_LAGS = (3, 6, 9)
AG_RELAYED = 6
RS_RELAYED = 6


def iota(shape, dim):
    return lax.broadcasted_iota(jnp.int32, shape, dim)


def remote(src, dst, send, recv, device):
    return pltpu.make_async_remote_copy(
        src_ref=src, dst_ref=dst, send_sem=send, recv_sem=recv, device_id=device, device_id_type=MESH
    )


def wait(ref, sem):
    pltpu.make_async_copy(ref, ref, sem).wait()


def kernel(
    q_ref, k_ref, v_ref, res_ref, wo_ref, gain_ref, rt_ref, ids_ref, wg_ref, wu_ref, wd_ref,
    att_out, mix_out,
    qv, kv, qs, top, tot, acc, attn, wo, res, wg, wu, wd,
    zs, zr, att, stats, place, perm, unperm, zunits,
    slots, scales, gate_acc, up_acc, hid, wgt_hi, wgt_lo,
    part, r1p, r1m, r2p, r2m, r2x, r4p, r4m, r4x, zout, fin, terms,
    ld, kvs, kvr, ws, wr, z1s, z1r, zas, zar, sts, str_, ats, atr, ags, agr, scs, scr, rss, rsr,
    z2s, z2r, outs,
):
    c = lax.axis_index("ctx")
    e = lax.axis_index("exp")
    core = lax.rem(c, 2)
    chip = lax.div(c, 2)
    x = lax.rem(chip, 4)
    y = lax.div(chip, 4)
    a = x + core * (y - x)
    b = y + core * (x - y)

    def ctx_of(aa, bb):
        return ((bb + core * (aa - bb)) * 4 + aa + core * (bb - aa)) * 2 + core

    ap, am, a2 = lax.rem(a + 1, 4), lax.rem(a + 3, 4), lax.rem(a + 2, 4)
    bp, bm, b2 = lax.rem(b + 1, 4), lax.rem(b + 3, 4), lax.rem(b + 2, 4)
    to_ap, to_am, to_a2 = (ctx_of(ap, b), e), (ctx_of(am, b), e), (ctx_of(a2, b), e)
    to_bp, to_bm, to_b2 = (ctx_of(a, bp), e), (ctx_of(a, bm), e), (ctx_of(a, b2), e)

    def chunk(s):
        return lax.rem(e + s + NZ, NZ)

    def to_z(s):
        return (c, chunk(s))

    to_sib = (c + 1 - 2 * core, e)

    loads = [
        pltpu.make_async_copy(q_ref, qv, ld.at[0]),
        pltpu.make_async_copy(wo_ref, wo, ld.at[1]),
        pltpu.make_async_copy(
            res_ref.at[:, pl.ds(pl.multiple_of(e * COLS, COLS), COLS)], res, ld.at[2]
        ),
        pltpu.make_async_copy(wg_ref.at[0], wg.at[0:FF], ld.at[3]),
        pltpu.make_async_copy(wu_ref.at[0], wu.at[0:FF], ld.at[4]),
        pltpu.make_async_copy(wd_ref.at[0], wd.at[0:FF], ld.at[5]),
    ]

    def kv_rows(kk, bb, aa, units=1):
        return pl.ds(pl.multiple_of((kk * NB + bb * 4 + aa) * TOK, TOK), units * TOK)

    own = kv_rows(core, b, a)
    own_k = pltpu.make_async_copy(k_ref, kv.at[own, 0:HEAD], ld.at[6])
    own_v = pltpu.make_async_copy(v_ref, kv.at[own, HEAD : 2 * HEAD], ld.at[7])

    steps = [(da, db) for db in (0, 1, 3, 2) for da in (0, 1, 3, 2) if da + db > 0]

    def at_step(da, db):
        return lax.rem(a + da, 4), lax.rem(b + db, 4)

    own_k.start()
    own_v.start()
    barrier = pltpu.get_barrier_semaphore()
    for da, db in steps:
        pl.semaphore_signal(
            barrier, inc=1, device_id=(ctx_of(*at_step(da, db)), e), device_id_type=MESH
        )
    for s in range(1, NZ):
        pl.semaphore_signal(barrier, inc=1, device_id=to_z(s), device_id_type=MESH)
    pl.semaphore_signal(barrier, inc=1, device_id=to_sib, device_id_type=MESH)
    loads[0].start()
    own_k.wait()
    own_v.wait()
    pl.semaphore_wait(barrier, len(steps) + NZ)

    mine_kv = kv.at[own, :]
    for i, (da, db) in enumerate(steps):
        device = (ctx_of(*at_step(da, db)), e)
        remote(mine_kv, mine_kv, kvs.at[i], kvr.at[db * 4 + da], device).start()
    for copy in loads[1:]:
        copy.start()

    ids = ids_ref[...]
    first_id, second_id = ids[0:1, :], ids[1:2, :]
    number = iota((NZ, TOK), 0)
    named = jnp.where((first_id == number) | (second_id == number), 1.0, 0.0)
    before = jnp.where(iota((TOK, TOK), 0) < iota((TOK, TOK), 1), 1.0, 0.0).astype(BF16)
    slot = jnp.dot(named.astype(BF16), before, preferred_element_type=F32)
    slot = jnp.where(named > 0.0, slot, -1.0)
    row = iota((2 * MAIN, TOK), 0)
    wanted = jnp.where(row < MAIN, row, MAIN + lax.rem(row, REM)).astype(F32)
    for k in range(NZ):
        here = jnp.broadcast_to(slot[k : k + 1, :], (2 * MAIN, TOK)) == wanted
        place[k * 2 * MAIN : (k + 1) * 2 * MAIN, :] = jnp.where(here, 1.0, 0.0).astype(BF16)
    my_slot = jnp.sum(jnp.where(number == e, slot, 0.0), axis=0, keepdims=True)
    by_token = jnp.where(
        jnp.broadcast_to(my_slot, (HEAD, TOK)) == iota((HEAD, TOK), 0).astype(F32), 1.0, 0.0
    ).astype(BF16)
    eye = jnp.where(iota((TOK, TOK), 0) == iota((TOK, TOK), 1), 1.0, 0.0)
    slot_of_token = lax.dot_general(eye.astype(BF16), by_token, NT, preferred_element_type=F32)

    r256, l256 = iota((256, 256), 0), iota((256, 256), 1)
    i64 = lax.rem(r256, 64)
    to_unit = lax.div(i64, REM) * 16 + lax.div(r256, 64) * REM + lax.rem(i64, REM)
    perm[...] = jnp.where(l256 == to_unit, 1.0, 0.0).astype(BF16)
    to_flat = lax.rem(lax.div(r256, REM), 4) * 64 + lax.div(r256, 16) * REM + lax.rem(r256, REM)
    unperm[...] = jnp.where(l256 == to_flat, 1.0, 0.0).astype(BF16)

    gate_acc[...] = jnp.zeros_like(gate_acc)
    up_acc[...] = jnp.zeros_like(up_acc)
    half = COLS // 2
    stats[e] = jnp.zeros((2 * NZ, 128), F32)
    top[...] = jnp.full(top.shape, -1e30, F32)
    tot[...] = jnp.zeros_like(tot)
    acc[...] = jnp.zeros_like(acc)

    loads[0].wait()
    for g in range(GROUPS):
        qs[g * TOK : (g + 1) * TOK, :] = qv[:, g * HEAD : (g + 1) * HEAD]

    klane, vlane = slice(0, HEAD), slice(HEAD, 2 * HEAD)

    def row_wait(db, bb):
        for da in range(4):
            if da + db > 0:
                wait(kv.at[kv_rows(core, bb, lax.rem(a + 4 - da, 4)), :], kvr.at[db * 4 + da])

    def row_pass(i, bb):
        rows = kv.at[kv_rows(core, bb, 0, 4), :]
        remote(rows, rows, kvs.at[15 + i], kvr.at[16 + i], to_sib).start()

    query_pos = c * TOK + lax.rem(iota((GROUPS * TOK, 1), 0), TOK)
    lane = iota((1, BUNDLE), 1)
    score_scale = 1.0 / math.sqrt(HEAD)

    def attend(kk, bb):
        rows = kv_rows(kk, bb, 0, 4)
        key_pos = (
            TOK * kk
            + lax.rem(lane, TOK)
            + 2 * TOK * ((1 + 3 * kk) * lax.div(lane, TOK) + (4 - 3 * kk) * bb)
        )
        scores = (
            lax.dot_general(qs[...], kv[rows, klane], NT, preferred_element_type=F32) * score_scale
        )
        allowed = key_pos <= query_pos
        if SEQ > WINDOW:
            allowed = allowed & (key_pos > query_pos - WINDOW)
        scores = jnp.where(allowed, scores, -1e30)
        old = top[:, 0:1]
        new = jnp.maximum(old, jnp.max(scores, axis=1, keepdims=True))
        fade = jnp.exp(old - new)
        weights = jnp.exp(scores - new)
        top[...] = jnp.broadcast_to(new, top.shape)
        tot[...] = tot[...] * fade + jnp.sum(weights, axis=1, keepdims=True)
        acc[...] = acc[...] * fade + jnp.dot(
            weights.astype(BF16), kv[rows, vlane], preferred_element_type=F32
        )

    def other_wait(i, aa):
        wait(kv.at[kv_rows(1 - core, aa, 0, 4), :], kvr.at[16 + i])

    row_wait(0, b)
    row_pass(0, b)
    attend(core, b)
    other_wait(0, a)
    attend(1 - core, a)
    row_wait(1, bm)
    row_pass(1, bm)
    row_wait(3, bp)
    row_pass(2, bp)
    attend(core, bm)
    attend(core, bp)
    row_wait(2, b2)
    row_pass(3, b2)
    for i, (src, dst) in enumerate(((wg_ref, wg), (wu_ref, wu), (wd_ref, wd))):
        remote(src.at[0], dst.at[FF : 2 * FF], ws.at[i], wr.at[i], to_sib).start()
    other_wait(1, am)
    attend(1 - core, am)
    other_wait(2, ap)
    attend(1 - core, ap)
    attend(core, b2)
    other_wait(3, a2)
    attend(1 - core, a2)

    for g in range(GROUPS):
        rows = slice(g * TOK, (g + 1) * TOK)
        attn[:, g * HEAD : (g + 1) * HEAD] = (acc[rows, :] / tot[rows, 0:1]).astype(BF16)

    def cols(j):
        return pl.ds(pl.multiple_of(j * COLS, COLS), COLS)

    def project(s):
        return jnp.dot(attn[...], wo[:, cols(chunk(s))], preferred_element_type=F32)

    lo, hi = slice(0, half), slice(half, COLS)
    full = slice(0, COLS)
    moves = (
        (0, lo, 0, 2), (0, hi, 7, -2), (1, full, 1, 1), (2, full, 2, -1), (3, full, 3, 1), (4, full, 4, -1),
        (5, full, 5, 2), (6, full, 6, -2),
    )

    def sum_send(k):
        i, lanes, sem, step = moves[k]
        remote(
            zs.at[i, :, lanes], zr.at[i, :, lanes], z1s.at[sem], z1r.at[sem], to_z(step)
        ).start()

    def sum_wait(k):
        i, lanes, sem, _ = moves[k]
        wait(zr.at[i, :, lanes], z1r.at[sem])

    loads[1].wait()
    zs[0] = project(4).astype(BF16)
    sum_send(0)
    sum_send(1)
    for i, s in ((1, 3), (2, -3), (3, 1), (4, -1)):
        zs[i] = project(s).astype(BF16)
        sum_send(i + 1)
    up, down = project(2), project(-2)
    loads[2].wait()
    total = project(0) + res[...].astype(F32)
    sum_wait(2)
    sum_wait(0)
    up = up + zr[1].astype(F32)
    zs[5, :, lo] = (up[:, lo] + zr[0, :, lo].astype(F32)).astype(BF16)
    zs[5, :, hi] = up[:, hi].astype(BF16)
    sum_send(6)
    sum_wait(3)
    sum_wait(1)
    down = down + zr[2].astype(F32)
    zs[6, :, hi] = (down[:, hi] + zr[0, :, hi].astype(F32)).astype(BF16)
    zs[6, :, lo] = down[:, lo].astype(BF16)
    sum_send(7)
    sum_wait(4)
    sum_wait(5)
    total = total + zr[3].astype(F32) + zr[4].astype(F32)
    sum_wait(6)
    sum_wait(7)
    total = (total + zr[5].astype(F32) + zr[6].astype(F32)).astype(BF16)
    att[e] = total

    def unit(aa, bb):
        return pl.ds(pl.multiple_of((bb * 4 + aa) * MAIN, MAIN), MAIN)

    tile = lax.div(iota((MAIN, 128), 0), REM)
    value = total.astype(F32)
    scaled = (value * gain_ref[:, cols(e)]).astype(BF16)
    packed = jnp.dot(place[...], scaled, preferred_element_type=F32)
    for k in range(NZ):
        at = k * 2 * MAIN
        zunits[k, :, 0:COLS] = packed[at : at + MAIN].astype(BF16)
        rest = jnp.zeros((MAIN, 128), F32)
        for t in range(4):
            rest = rest + jnp.where(
                tile == t, packed[at + MAIN : at + 2 * MAIN, t * 128 : (t + 1) * 128], 0.0
            )
        zunits[k, :, COLS:UNIT] = rest.astype(BF16)
    spread_steps = ((1, 2), (-1, 1), (2, 4), (-2, 3), (3, 6), (-3, 5), (4, 7))
    for s, n in spread_steps:
        remote(
            zunits.at[chunk(s)], slots.at[e, unit(a, b), :], zas.at[n], zar.at[n], to_z(s)
        ).start()
    slots[e, unit(a, b), :] = zunits[e]
    squares = jnp.sum(value * value, axis=1, keepdims=True)
    stats[e, 0:NZ, 0:TOK] = lax.dot_general(
        rt_ref[:, cols(e)], scaled, NT, preferred_element_type=F32
    )
    stats[e, NZ : 2 * NZ, 0:TOK] = jnp.broadcast_to(
        jnp.sum(eye * squares, axis=0, keepdims=True), (NZ, TOK)
    )

    def ag_chunk(n):
        odd = lax.rem(n, 2)
        return chunk((2 * odd - 1) * lax.div(n + 1, 2))

    def bundle(bb):
        return pl.ds(pl.multiple_of(bb * 64, 64), 64)

    def first_half(bb):
        return pl.ds(pl.multiple_of(bb * 64, 32), 32)

    def second_half(bb):
        return pl.ds(pl.multiple_of(bb * 64 + 32, 32), 32)

    def scale_unit(aa, bb):
        return pl.ds(pl.multiple_of((bb * 4 + aa) * 8, 8), 8)

    def scale_bundle(bb):
        return pl.ds(pl.multiple_of(bb * 32, 8), 32)

    def out_copy(j):
        return pltpu.make_async_copy(att.at[j], att_out.at[:, cols(j)], outs.at[j])

    def token_stats():
        whole = stats[0]
        for k in range(1, NZ):
            whole = whole + stats[k]
        inverse = lax.rsqrt(whole[NZ : NZ + 1, 0:TOK] * (1.0 / D) + 1e-05)
        return whole[0:NZ, 0:TOK] * inverse, inverse

    def ag_start(n):
        j = ag_chunk(n)
        here = slots.at[j, unit(a, b), :]

        @pl.when(n > 0)
        def _():
            wait(here, zar.at[n])

        remote(here, here, ags.at[0, n], agr.at[0, n], to_ap).start()
        remote(here, here, ags.at[1, n], agr.at[1, n], to_am).start()
        remote(here, here, ags.at[2, n], agr.at[2, n], to_a2).start()

        @pl.when(n == 0)
        def _():
            for s, k in spread_steps:
                remote(stats.at[e], stats.at[e], sts.at[k], str_.at[k], to_z(s)).start()
            for s, k in spread_steps:
                remote(att.at[e], att.at[e], ats.at[k], atr.at[k], to_z(s)).start()

        @pl.when(n == 7)
        def _():
            for k in range(1, NZ):
                wait(stats.at[ag_chunk(k)], str_.at[k])
            inverse = token_stats()[1]
            inverse = jnp.sum(eye * inverse, axis=1, keepdims=True)
            by_slot = jnp.sum(slot_of_token * inverse, axis=0, keepdims=True)
            scales[scale_unit(a, b), :] = jnp.broadcast_to(by_slot, (8, HEAD))
            here = scales.at[scale_unit(a, b), :]
            remote(here, here, scs.at[0], scr.at[0], to_ap).start()
            remote(here, here, scs.at[1], scr.at[1], to_am).start()
            remote(here, here, scs.at[2], scr.at[2], to_a2).start()

    def ag_second(n):
        j = ag_chunk(n)
        wait(slots.at[j, unit(am, b), :], agr.at[0, n])
        wait(slots.at[j, unit(ap, b), :], agr.at[1, n])
        wait(slots.at[j, unit(a2, b), :], agr.at[2, n])
        piece = slots.at[j, bundle(b), :]
        remote(piece, piece, ags.at[3, n], agr.at[3, n], to_bp).start()
        remote(piece, piece, ags.at[4, n], agr.at[4, n], to_bm).start()

        @pl.when(n >= AG_RELAYED)
        def _():
            remote(piece, piece, ags.at[5, n], agr.at[5, n], to_b2).start()

        @pl.when(n == 7)
        def _():
            wait(scales.at[scale_unit(am, b), :], scr.at[0])
            wait(scales.at[scale_unit(ap, b), :], scr.at[1])
            wait(scales.at[scale_unit(a2, b), :], scr.at[2])
            piece = scales.at[scale_bundle(b), :]
            remote(piece, piece, scs.at[3], scr.at[3], to_bp).start()
            remote(piece, piece, scs.at[4], scr.at[4], to_bm).start()
            remote(piece, piece, scs.at[5], scr.at[5], to_b2).start()

    def ag_third(n):
        j = ag_chunk(n)

        @pl.when(n < AG_RELAYED)
        def _():
            wait(slots.at[j, bundle(bm), :], agr.at[3, n])
            piece = slots.at[j, first_half(bm), :]
            remote(piece, piece, ags.at[5, n], agr.at[5, n], to_bp).start()
            wait(slots.at[j, bundle(bp), :], agr.at[4, n])
            piece = slots.at[j, second_half(bp), :]
            remote(piece, piece, ags.at[6, n], agr.at[6, n], to_bm).start()

    def ag_use(n):
        j = ag_chunk(n)

        @pl.when(n < AG_RELAYED)
        def _():
            wait(slots.at[j, first_half(b2), :], agr.at[5, n])
            wait(slots.at[j, second_half(b2), :], agr.at[6, n])

        @pl.when(n >= AG_RELAYED)
        def _():
            wait(slots.at[j, bundle(bm), :], agr.at[3, n])
            wait(slots.at[j, bundle(bp), :], agr.at[4, n])
            wait(slots.at[j, bundle(b2), :], agr.at[5, n])

        flat = jnp.dot(
            perm[...], slots[j, 0:256, COLS:UNIT], preferred_element_type=F32
        ).astype(BF16)
        for t in range(4):
            slots[j, 256:ROWS, t * 128 : (t + 1) * 128] = flat[t * 64 : (t + 1) * 64]
        rows = slots[j, :, 0:COLS]
        gate_acc[...] += lax.dot_general(rows, wg[:, cols(j)], NT, preferred_element_type=F32)
        up_acc[...] += lax.dot_general(rows, wu[:, cols(j)], NT, preferred_element_type=F32)

    def run(stages, count):
        last = max(lag for _, lag in stages)

        def tick(t, carry):
            for function, lag in stages:

                @pl.when((t >= lag) & (t < lag + count))
                def _(function=function, lag=lag):
                    function(t - lag)

            return carry

        lax.fori_loop(0, count + last, tick, 0)

    loads[3].wait()
    loads[4].wait()
    wait(wg.at[FF : 2 * FF], wr.at[0])
    wait(wu.at[FF : 2 * FF], wr.at[1])
    run(((ag_third, AG_LAGS[1]), (ag_second, AG_LAGS[0]), (ag_start, 0), (ag_use, AG_LAGS[2])), NZ)
    wait(scales.at[scale_bundle(bm), :], scr.at[3])
    wait(scales.at[scale_bundle(bp), :], scr.at[4])
    wait(scales.at[scale_bundle(b2), :], scr.at[5])

    row = iota((ROWS, HEAD), 0)
    col = iota((ROWS, HEAD), 1)
    over = row - 256
    block_of = jnp.where(row < 256, lax.div(row, MAIN), lax.div(over, REM))
    slot_of = jnp.where(row < 256, lax.rem(row, MAIN), MAIN + lax.rem(over + 256, REM))
    pick = jnp.where(col == block_of * 8, 1.0, 0.0)
    spread = jnp.dot(pick, scales[...], precision=HIGH, preferred_element_type=F32)
    factor = jnp.sum(jnp.where(col == slot_of, spread, 0.0), axis=1, keepdims=True)
    gated = gate_acc[...] * factor
    hid[...] = (gated / (1.0 + jnp.exp(-gated)) * (up_acc[...] * factor)).astype(BF16)
    loads[5].wait()
    wait(wd.at[FF : 2 * FF], wr.at[2])

    def rs_chunk(n):
        odd = lax.rem(n, 2)
        return chunk(odd * (4 - lax.div(n + 1, 2)) - (1 - odd) * (4 - lax.div(n, 2)))

    def rs_start(n):
        j = rs_chunk(n)
        out = jnp.dot(hid[...], wd[:, cols(j)], preferred_element_type=F32).astype(BF16)
        part[n, :, 0:COLS] = out[0:256]
        rest = jnp.concatenate([out[256:, t * 128 : (t + 1) * 128] for t in range(4)], axis=0)
        part[n, :, COLS:UNIT] = jnp.dot(unperm[...], rest, preferred_element_type=F32).astype(BF16)

        @pl.when(n < RS_RELAYED)
        def _():
            remote(
                part.at[n, first_half(b2), :], r1p.at[n], rss.at[0, n], rsr.at[0, n], to_bp
            ).start()
            remote(
                part.at[n, second_half(b2), :], r1m.at[n], rss.at[1, n], rsr.at[1, n], to_bm
            ).start()

        @pl.when(n >= RS_RELAYED)
        def _():
            remote(part.at[n, bundle(b2), :], r2x.at[n], rss.at[0, n], rsr.at[0, n], to_b2).start()
            remote(part.at[n, bundle(bp), :], r2p.at[n], rss.at[2, n], rsr.at[2, n], to_bp).start()
            remote(part.at[n, bundle(bm), :], r2m.at[n], rss.at[3, n], rsr.at[3, n], to_bm).start()

        @pl.when(n > 0)
        def _():
            wait(att.at[ag_chunk(n)], atr.at[n])

        out_copy(ag_chunk(n)).start()

        @pl.when(n == 7)
        def _():
            logits = token_stats()[0]
            one = jnp.sum(jnp.where(number == first_id, logits, 0.0), axis=0, keepdims=True)
            two = jnp.sum(jnp.where(number == second_id, logits, 0.0), axis=0, keepdims=True)
            gate = 1.0 / (1.0 + jnp.exp(two - one))
            gates = jnp.where(first_id == number, gate, 1.0 - gate)
            spread = jnp.concatenate(
                [jnp.broadcast_to(gates[k : k + 1, :], (2 * MAIN, TOK)) for k in range(NZ)], axis=0
            )
            spread = spread * place[...].astype(F32)
            turned = lax.dot_general(eye, spread, NT, precision=HIGH, preferred_element_type=F32)
            high = turned.astype(BF16)
            wgt_hi[...] = high
            wgt_lo[...] = (turned - high.astype(F32)).astype(BF16)

    def add(n, rows, lanes, more):
        value = part[n, rows, lanes].astype(F32)
        for term in more:
            value = value + term.astype(F32)
        return value

    every = slice(0, UNIT)

    def rs_first(n):
        @pl.when(n < RS_RELAYED)
        def _():
            wait(r1p.at[n], rsr.at[0, n])
            rows = first_half(bp)
            part[n, rows, every] = add(n, rows, every, [r1p[n]]).astype(BF16)
            remote(part.at[n, bundle(bp), :], r2p.at[n], rss.at[2, n], rsr.at[2, n], to_bp).start()
            wait(r1m.at[n], rsr.at[1, n])
            rows = second_half(bm)
            part[n, rows, every] = add(n, rows, every, [r1m[n]]).astype(BF16)
            remote(part.at[n, bundle(bm), :], r2m.at[n], rss.at[3, n], rsr.at[3, n], to_bm).start()

    def rs_second(n):
        wait(r2p.at[n], rsr.at[2, n])
        wait(r2m.at[n], rsr.at[3, n])
        rows = bundle(b)

        @pl.when(n < RS_RELAYED)
        def _():
            part[n, rows, every] = add(n, rows, every, [r2p[n], r2m[n]]).astype(BF16)

        @pl.when(n >= RS_RELAYED)
        def _():
            wait(r2x.at[n], rsr.at[0, n])
            part[n, rows, every] = add(n, rows, every, [r2p[n], r2m[n], r2x[n]]).astype(BF16)

        remote(part.at[n, unit(a2, b), :], r4x.at[n], rss.at[4, n], rsr.at[4, n], to_a2).start()
        remote(part.at[n, unit(ap, b), :], r4p.at[n], rss.at[5, n], rsr.at[5, n], to_ap).start()
        remote(part.at[n, unit(am, b), :], r4m.at[n], rss.at[6, n], rsr.at[6, n], to_am).start()

    def rs_last(n):
        wait(r4p.at[n], rsr.at[5, n])
        wait(r4m.at[n], rsr.at[6, n])
        wait(r4x.at[n], rsr.at[4, n])
        zout[n] = add(n, unit(a, b), every, [r4p[n], r4m[n], r4x[n]]).astype(BF16)

        @pl.when(n < 7)
        def _():
            remote(zout.at[n], fin.at[e], z2s.at[n], z2r.at[7 - n], (c, rs_chunk(n))).start()

        @pl.when(n == 7)
        def _():
            fin[e] = zout[7]

    run(((rs_last, RS_LAGS[2]), (rs_second, RS_LAGS[1]), (rs_first, RS_LAGS[0]), (rs_start, 0)), NZ)

    for n in range(1, NZ):
        wait(fin.at[ag_chunk(n)], z2r.at[n])
    for k in range(NZ):
        at = k * 2 * MAIN
        terms[at : at + MAIN, :] = fin[k, :, 0:COLS]
        rest = fin[k, :, COLS:UNIT].astype(F32)
        for t in range(4):
            terms[at + MAIN : at + 2 * MAIN, t * 128 : (t + 1) * 128] = jnp.where(
                tile == t, rest, 0.0
            ).astype(BF16)
    mixed = jnp.dot(wgt_hi[...], terms[...], preferred_element_type=F32)
    mixed = mixed + jnp.dot(wgt_lo[...], terms[...], preferred_element_type=F32)
    mix_out[...] = mixed.astype(BF16)

    for i in range(15):
        wait(mine_kv, kvs.at[i])
    for i in range(4):
        wait(kv.at[0 : 4 * TOK, :], kvs.at[15 + i])
    for i, ref in enumerate((wg, wu, wd)):
        wait(ref.at[FF : 2 * FF], ws.at[i])
    for i, lanes, sem, _ in moves:
        wait(zs.at[i, :, lanes], z1s.at[sem])

    def drain(n, carry):
        for i, rows in enumerate((MAIN, MAIN, MAIN, 64, 64)):
            wait(slots.at[0, 0:rows, :], ags.at[i, n])

        @pl.when(n < AG_RELAYED)
        def _():
            wait(slots.at[0, 0:32, :], ags.at[5, n])
            wait(slots.at[0, 0:32, :], ags.at[6, n])

        @pl.when(n >= AG_RELAYED)
        def _():
            wait(slots.at[0, 0:64, :], ags.at[5, n])

        @pl.when(n < RS_RELAYED)
        def _():
            wait(r1p.at[0], rss.at[0, n])
            wait(r1p.at[0], rss.at[1, n])

        @pl.when(n >= RS_RELAYED)
        def _():
            wait(r2x.at[0], rss.at[0, n])

        for i, piece in ((2, r2p), (3, r2m), (4, r4x), (5, r4p), (6, r4m)):
            wait(piece.at[0], rss.at[i, n])

        @pl.when(n < 7)
        def _():
            wait(zout.at[0], z2s.at[n])
            wait(zunits.at[0], zas.at[n + 1])
            wait(stats.at[0], sts.at[n + 1])
            wait(att.at[0], ats.at[n + 1])

        out_copy(n).wait()
        return carry

    lax.fori_loop(0, NZ, drain, 0)
    for i in range(6):
        wait(scales.at[0:8, :] if i < 3 else scales.at[0:32, :], scs.at[i])


def local(
    query, key_states, value_states, residual, out_weight, norm_gain, router_weight, expert_ids,
    gate_weight, up_weight, down_weight,
):
    anywhere = pl.BlockSpec(memory_space=pl.ANY)
    near = pl.BlockSpec(memory_space=pltpu.VMEM)
    vmem = pltpu.VMEM
    dma = pltpu.SemaphoreType.DMA
    scratch = [
        vmem((TOK, GROUPS * HEAD), BF16),
        vmem((SEQ, 2 * HEAD), BF16),
        vmem((GROUPS * TOK, HEAD), BF16),
        vmem((GROUPS * TOK, HEAD), F32),
        vmem((GROUPS * TOK, HEAD), F32),
        vmem((GROUPS * TOK, HEAD), F32),
        vmem((TOK, GROUPS * HEAD), BF16),
        vmem((GROUPS * HEAD, D), BF16),
        vmem((TOK, COLS), BF16),
        vmem((2 * FF, D), BF16),
        vmem((2 * FF, D), BF16),
        vmem((2 * FF, D), BF16),
        vmem((7, TOK, COLS), BF16),
        vmem((7, TOK, COLS), BF16),
        vmem((NZ, TOK, COLS), BF16),
        vmem((NZ, 2 * NZ, 128), F32),
        vmem((NZ * 2 * MAIN, TOK), BF16),
        vmem((256, 256), BF16),
        vmem((256, 256), BF16),
        vmem((NZ, MAIN, UNIT), BF16),
        vmem((NZ, ROWS, UNIT), BF16),
        vmem((NB * 8, HEAD), F32),
        vmem((ROWS, 2 * FF), F32),
        vmem((ROWS, 2 * FF), F32),
        vmem((ROWS, 2 * FF), BF16),
        vmem((TOK, NZ * 2 * MAIN), BF16),
        vmem((TOK, NZ * 2 * MAIN), BF16),
        vmem((NZ, 256, UNIT), BF16),
        vmem((NZ, 32, UNIT), BF16),
        vmem((NZ, 32, UNIT), BF16),
        vmem((NZ, 64, UNIT), BF16),
        vmem((NZ, 64, UNIT), BF16),
        vmem((NZ, 64, UNIT), BF16),
        vmem((NZ, MAIN, UNIT), BF16),
        vmem((NZ, MAIN, UNIT), BF16),
        vmem((NZ, MAIN, UNIT), BF16),
        vmem((NZ, MAIN, UNIT), BF16),
        vmem((NZ, MAIN, UNIT), BF16),
        vmem((NZ * 2 * MAIN, COLS), BF16),
        dma((8,)),
        dma((19,)),
        dma((20,)),
        dma((3,)),
        dma((3,)),
        dma((8,)),
        dma((8,)),
        dma((8,)),
        dma((8,)),
        dma((8,)),
        dma((8,)),
        dma((8,)),
        dma((8,)),
        dma((7, NZ)),
        dma((7, NZ)),
        dma((6,)),
        dma((6,)),
        dma((7, NZ)),
        dma((7, NZ)),
        dma((8,)),
        dma((8,)),
        dma((NZ,)),
    ]
    return pl.pallas_call(
        kernel,
        out_shape=(
            jax.ShapeDtypeStruct((TOK, D), BF16),
            jax.ShapeDtypeStruct((TOK, COLS), BF16),
        ),
        in_specs=[anywhere] * 5 + [near] * 3 + [anywhere] * 3,
        out_specs=(anywhere, near),
        scratch_shapes=scratch,
        compiler_params=pltpu.CompilerParams(
            collective_id=0, has_side_effects=True, vmem_limit_bytes=56 * 1024 * 1024
        ),
        name="layer",
    )(
        query,
        key_states,
        value_states,
        residual,
        out_weight,
        norm_gain.reshape(1, D),
        router_weight.T,
        expert_ids.T,
        jnp.swapaxes(gate_weight, 1, 2),
        jnp.swapaxes(up_weight, 1, 2),
        down_weight,
    )


def solution(mesh):
    placed = (
        P("ctx", "exp"),
        P("ctx", "exp"),
        P("ctx", "exp"),
        P("ctx", None),
        P("exp", None),
        P(),
        P(),
        P("ctx", None),
        P("exp", None, "ctx"),
        P("exp", None, "ctx"),
        P("exp", "ctx", None),
    )
    return jax.shard_map(
        local,
        mesh=mesh,
        in_specs=placed,
        out_specs=(P("ctx", None), P("ctx", "exp")),
        check_vma=False,
    )
```

time: 140 us -> 93.6 us (0.67)
  Pallas kernels: 135 us -> 89.3 us
    pallas_call x1, Pallas kernels: 135 us -> 89.3 us  [local(): pl.pallas_call(kernel, out_shape=(jax.ShapeDtypeStruct((TOK, D), BF16), j...]
where the time goes in v2:
time: 93.6 us; the launch traced here: 93.3 us
  Pallas kernels  89.3 us (95%)
  local copies, waits for them, and re-layouts  3.34 us (4%)
    pallas_call x1, Pallas kernels, local(): pl.pallas_call(kernel, out_shape=(jax.ShapeDtypeStruct((TOK, D), BF16), j...  89.3 us
    unnamed x2, local copies, waits for them, and re-layouts  3.34 us

profile of v2, /device:TPU:8, one launch (start us, length us, event | category | flops | bytes accessed | tf_op | source)
XLA Modules:
  0.0 93.3 jit_solution(14153858693588106046)
XLA Ops:
  0.6 89.3 %layer.1 = (bf16[64,4096]{1,0:T(8,128)(2,1)}, bf16[64,512]{1,0:T(8,128)(2,1)}) custom-call(bf16[64,512]{1,0:T(8,128)(2,1)} %q_ref.1, bf16[64,128]{1,0:T(8,128)(2,1)} %k_ref.1, bf16[64,128]{1,0:T(8,128)(2,1)} %v_ref.1, bf16[64,4096]{1,0:T(8,128)(2,1)} %res_ref.1, bf16[512,4096]{1,0:T(8,128)(2,1)} %wo_ref.1, f32[1,4096]{1,0:T(1,128)} %bitcast.8, ...), custom_call_target="tpu_custom_call" | custom-call | tf_op jit(solution)/shard_map/layer/pallas_call | solution.py:714
  90.0 1.9 %copy.15 = bf16[64,4096]{1,0:T(8,128)(2,1)} copy(bf16[64,4096]{1,0:T(8,128)(2,1)} %get-tuple-element.4) | data formatting | bytes 1048576
  91.8 1.5 %copy.16 = bf16[64,512]{1,0:T(8,128)(2,1)} copy(bf16[64,512]{1,0:T(8,128)(2,1)} %get-tuple-element.5) | data formatting | bytes 131072

commit v3 on v2

--- a/solution.py
+++ b/solution.py
@@ -30,10 +30,9 @@
 HIGH = lax.Precision.HIGHEST
 NT = (((1,), (1,)), ((), ()))
 
-AG_LAGS = (3, 6, 9)
 RS_LAGS = (3, 6, 9)
-AG_RELAYED = 6
-RS_RELAYED = 6
+AG_RELAYED = 8
+RS_RELAYED = 8
 
 
 def iota(shape, dim):
@@ -51,13 +50,13 @@
 
 
 def kernel(
-    q_ref, k_ref, v_ref, res_ref, wo_ref, gain_ref, rt_ref, ids_ref, wg_ref, wu_ref, wd_ref,
+    q_ref, k_ref, v_ref, res_ref, wo_ref, gain_hbm, rt_hbm, ids_hbm, wg_ref, wu_ref, wd_ref,
     att_out, mix_out,
-    qv, kv, qs, top, tot, acc, attn, wo, res, wg, wu, wd,
+    gain_ref, rt_ref, ids_ref, mixed_out, qv, kv, qs, top, tot, acc, attn, wo, res, wg, wu, wd,
     zs, zr, att, stats, place, perm, unperm, zunits,
     slots, scales, gate_acc, up_acc, hid, wgt_hi, wgt_lo,
     part, r1p, r1m, r2p, r2m, r2x, r4p, r4m, r4x, zout, fin, terms,
-    ld, kvs, kvr, ws, wr, z1s, z1r, zas, zar, sts, str_, ats, atr, ags, agr, scs, scr, rss, rsr,
+    ld, kvs, kvr, ws, wr, z1s, z1r, zas, zar, dis, dir_, sts, str_, ats, atr, ags, agr, scs, scr, rss, rsr,
     z2s, z2r, outs,
 ):
     c = lax.axis_index("ctx")
@@ -94,6 +93,8 @@
         pltpu.make_async_copy(wg_ref.at[0], wg.at[0:FF], ld.at[3]),
         pltpu.make_async_copy(wu_ref.at[0], wu.at[0:FF], ld.at[4]),
         pltpu.make_async_copy(wd_ref.at[0], wd.at[0:FF], ld.at[5]),
+        pltpu.make_async_copy(gain_hbm, gain_ref, ld.at[8]),
+        pltpu.make_async_copy(rt_hbm, rt_ref, ld.at[9]),
     ]
 
     def kv_rows(kk, bb, aa, units=1):
@@ -108,6 +109,7 @@
     def at_step(da, db):
         return lax.rem(a + da, 4), lax.rem(b + db, 4)
 
+    own_ids = pltpu.make_async_copy(ids_hbm, ids_ref, ld.at[10])
     own_k.start()
     own_v.start()
     barrier = pltpu.get_barrier_semaphore()
@@ -118,10 +120,15 @@
     for s in range(1, NZ):
         pl.semaphore_signal(barrier, inc=1, device_id=to_z(s), device_id_type=MESH)
     pl.semaphore_signal(barrier, inc=1, device_id=to_sib, device_id_type=MESH)
+    for s in (1, -1):
+        for da in (1, 2, 3):
+            other = (ctx_of(*at_step(da, 0)), chunk(s))
+            pl.semaphore_signal(barrier, inc=1, device_id=other, device_id_type=MESH)
     loads[0].start()
+    own_ids.start()
     own_k.wait()
     own_v.wait()
-    pl.semaphore_wait(barrier, len(steps) + NZ)
+    pl.semaphore_wait(barrier, len(steps) + NZ + 6)
 
     mine_kv = kv.at[own, :]
     for i, (da, db) in enumerate(steps):
@@ -130,6 +137,7 @@
     for copy in loads[1:]:
         copy.start()
 
+    own_ids.wait()
     ids = ids_ref[...]
     first_id, second_id = ids[0:1, :], ids[1:2, :]
     number = iota((NZ, TOK), 0)
@@ -290,6 +298,8 @@
     total = (total + zr[5].astype(F32) + zr[6].astype(F32)).astype(BF16)
     att[e] = total
 
+    loads[6].wait()
+    loads[7].wait()
     def unit(aa, bb):
         return pl.ds(pl.multiple_of((bb * 4 + aa) * MAIN, MAIN), MAIN)
 
@@ -307,11 +317,20 @@
             )
         zunits[k, :, COLS:UNIT] = rest.astype(BF16)
     spread_steps = ((1, 2), (-1, 1), (2, 4), (-2, 3), (3, 6), (-3, 5), (4, 7))
+    first_steps = ((1, 0), (3, 1), (2, 2))
+    mine_rows = unit(a, b)
     for s, n in spread_steps:
-        remote(
-            zunits.at[chunk(s)], slots.at[e, unit(a, b), :], zas.at[n], zar.at[n], to_z(s)
-        ).start()
-    slots[e, unit(a, b), :] = zunits[e]
+        src, dst = zunits.at[chunk(s)], slots.at[e, mine_rows, :]
+        remote(src, dst, zas.at[n], zar.at[n], to_z(s)).start()
+        if n < 3:
+            for da, i in first_steps:
+                device = (ctx_of(*at_step(da, 0)), chunk(s))
+                remote(src, dst, ags.at[i, n], agr.at[i, n], device).start()
+    slots[e, mine_rows, :] = zunits[e]
+    for i, (da, db) in enumerate(steps):
+        device = (ctx_of(*at_step(da, db)), e)
+        here = slots.at[e, mine_rows, :]
+        remote(here, here, dis.at[i], dir_.at[db * 4 + da], device).start()
     squares = jnp.sum(value * value, axis=1, keepdims=True)
     stats[e, 0:NZ, 0:TOK] = lax.dot_general(
         rt_ref[:, cols(e)], scaled, NT, preferred_element_type=F32
@@ -349,40 +368,46 @@
         inverse = lax.rsqrt(whole[NZ : NZ + 1, 0:TOK] * (1.0 / D) + 1e-05)
         return whole[0:NZ, 0:TOK] * inverse, inverse
 
+    def stats_send():
+        for s, k in spread_steps:
+            remote(stats.at[e], stats.at[e], sts.at[k], str_.at[k], to_z(s)).start()
+
+    def columns_send():
+        for s, k in spread_steps:
+            remote(att.at[e], att.at[e], ats.at[k], atr.at[k], to_z(s)).start()
+
     def ag_start(n):
-        j = ag_chunk(n)
-        here = slots.at[j, unit(a, b), :]
-
-        @pl.when(n > 0)
-        def _():
-            wait(here, zar.at[n])
-
+        here = slots.at[ag_chunk(n), mine_rows, :]
+        wait(here, zar.at[n])
         remote(here, here, ags.at[0, n], agr.at[0, n], to_ap).start()
         remote(here, here, ags.at[1, n], agr.at[1, n], to_am).start()
         remote(here, here, ags.at[2, n], agr.at[2, n], to_a2).start()
 
-        @pl.when(n == 0)
-        def _():
-            for s, k in spread_steps:
-                remote(stats.at[e], stats.at[e], sts.at[k], str_.at[k], to_z(s)).start()
-            for s, k in spread_steps:
-                remote(att.at[e], att.at[e], ats.at[k], atr.at[k], to_z(s)).start()
-
-        @pl.when(n == 7)
-        def _():
-            for k in range(1, NZ):
-                wait(stats.at[ag_chunk(k)], str_.at[k])
-            inverse = token_stats()[1]
-            inverse = jnp.sum(eye * inverse, axis=1, keepdims=True)
-            by_slot = jnp.sum(slot_of_token * inverse, axis=0, keepdims=True)
-            scales[scale_unit(a, b), :] = jnp.broadcast_to(by_slot, (8, HEAD))
-            here = scales.at[scale_unit(a, b), :]
-            remote(here, here, scs.at[0], scr.at[0], to_ap).start()
-            remote(here, here, scs.at[1], scr.at[1], to_am).start()
-            remote(here, here, scs.at[2], scr.at[2], to_a2).start()
+    def scale_start():
+        for k in range(1, NZ):
+            wait(stats.at[ag_chunk(k)], str_.at[k])
+        inverse = token_stats()[1]
+        inverse = jnp.sum(eye * inverse, axis=1, keepdims=True)
+        by_slot = jnp.sum(slot_of_token * inverse, axis=0, keepdims=True)
+        scales[scale_unit(a, b), :] = jnp.broadcast_to(by_slot, (8, HEAD))
+        here = scales.at[scale_unit(a, b), :]
+        remote(here, here, scs.at[0], scr.at[0], to_ap).start()
+        remote(here, here, scs.at[1], scr.at[1], to_am).start()
+        remote(here, here, scs.at[2], scr.at[2], to_a2).start()
+
+    def scale_second():
+        wait(scales.at[scale_unit(am, b), :], scr.at[0])
+        wait(scales.at[scale_unit(ap, b), :], scr.at[1])
+        wait(scales.at[scale_unit(a2, b), :], scr.at[2])
+        piece = scales.at[scale_bundle(b), :]
+        remote(piece, piece, scs.at[3], scr.at[3], to_bp).start()
+        remote(piece, piece, scs.at[4], scr.at[4], to_bm).start()
+        remote(piece, piece, scs.at[5], scr.at[5], to_b2).start()
 
     def ag_second(n):
         j = ag_chunk(n)
+        if isinstance(n, int) and n < 3:
+            wait(slots.at[j, mine_rows, :], zar.at[n])
         wait(slots.at[j, unit(am, b), :], agr.at[0, n])
         wait(slots.at[j, unit(ap, b), :], agr.at[1, n])
         wait(slots.at[j, unit(a2, b), :], agr.at[2, n])
@@ -394,32 +419,26 @@
         def _():
             remote(piece, piece, ags.at[5, n], agr.at[5, n], to_b2).start()
 
-        @pl.when(n == 7)
-        def _():
-            wait(scales.at[scale_unit(am, b), :], scr.at[0])
-            wait(scales.at[scale_unit(ap, b), :], scr.at[1])
-            wait(scales.at[scale_unit(a2, b), :], scr.at[2])
-            piece = scales.at[scale_bundle(b), :]
-            remote(piece, piece, scs.at[3], scr.at[3], to_bp).start()
-            remote(piece, piece, scs.at[4], scr.at[4], to_bm).start()
-            remote(piece, piece, scs.at[5], scr.at[5], to_b2).start()
-
     def ag_third(n):
         j = ag_chunk(n)
 
-        @pl.when(n < AG_RELAYED)
-        def _():
-            wait(slots.at[j, bundle(bm), :], agr.at[3, n])
-            piece = slots.at[j, first_half(bm), :]
-            remote(piece, piece, ags.at[5, n], agr.at[5, n], to_bp).start()
-            wait(slots.at[j, bundle(bp), :], agr.at[4, n])
-            piece = slots.at[j, second_half(bp), :]
-            remote(piece, piece, ags.at[6, n], agr.at[6, n], to_bm).start()
+        wait(slots.at[j, bundle(bm), :], agr.at[3, n])
+        piece = slots.at[j, first_half(bm), :]
+        remote(piece, piece, ags.at[5, n], agr.at[5, n], to_bp).start()
+        wait(slots.at[j, bundle(bp), :], agr.at[4, n])
+        piece = slots.at[j, second_half(bp), :]
+        remote(piece, piece, ags.at[6, n], agr.at[6, n], to_bm).start()
 
     def ag_use(n):
         j = ag_chunk(n)
 
-        @pl.when(n < AG_RELAYED)
+        @pl.when(n == 0)
+        def _():
+            for da, db in steps:
+                rows = unit(lax.rem(a + 4 - da, 4), lax.rem(b + 4 - db, 4))
+                wait(slots.at[j, rows, :], dir_.at[db * 4 + da])
+
+        @pl.when((n > 0) & (n < AG_RELAYED))
         def _():
             wait(slots.at[j, first_half(b2), :], agr.at[5, n])
             wait(slots.at[j, second_half(b2), :], agr.at[6, n])
@@ -453,11 +472,42 @@
 
         lax.fori_loop(0, count + last, tick, 0)
 
+    stats_send()
+    ag_second(1)
+    ag_start(3)
+    ag_start(4)
+    ag_second(2)
+    ag_start(5)
+    ag_start(6)
+    ag_start(7)
+    ag_second(3)
+    ag_third(1)
+    ag_second(4)
+    ag_third(2)
+    ag_second(5)
+    ag_second(6)
+    ag_second(7)
+    scale_start()
+    columns_send()
+
     loads[3].wait()
     loads[4].wait()
     wait(wg.at[FF : 2 * FF], wr.at[0])
     wait(wu.at[FF : 2 * FF], wr.at[1])
-    run(((ag_third, AG_LAGS[1]), (ag_second, AG_LAGS[0]), (ag_start, 0), (ag_use, AG_LAGS[2])), NZ)
+    def ag_tick(n, carry):
+        @pl.when((n > 0) & (n + 2 < AG_RELAYED))
+        def _():
+            ag_third(n + 2)
+
+        ag_use(n)
+
+        @pl.when(n == 2)
+        def _():
+            scale_second()
+
+        return carry
+
+    lax.fori_loop(0, NZ, ag_tick, 0)
     wait(scales.at[scale_bundle(bm), :], scr.at[3])
     wait(scales.at[scale_bundle(bp), :], scr.at[4])
     wait(scales.at[scale_bundle(b2), :], scr.at[5])
@@ -575,7 +625,8 @@
         def _():
             fin[e] = zout[7]
 
-    run(((rs_last, RS_LAGS[2]), (rs_second, RS_LAGS[1]), (rs_first, RS_LAGS[0]), (rs_start, 0)), NZ)
+    run(((rs_start, 0),), NZ)
+    run(((rs_last, 10), (rs_second, 6), (rs_first, 0)), NZ)
 
     for n in range(1, NZ):
         wait(fin.at[ag_chunk(n)], z2r.at[n])
@@ -589,7 +640,9 @@
             ).astype(BF16)
     mixed = jnp.dot(wgt_hi[...], terms[...], preferred_element_type=F32)
     mixed = mixed + jnp.dot(wgt_lo[...], terms[...], preferred_element_type=F32)
-    mix_out[...] = mixed.astype(BF16)
+    mixed_out[...] = mixed.astype(BF16)
+    mix_copy = pltpu.make_async_copy(mixed_out, mix_out, ld.at[11])
+    mix_copy.start()
 
     for i in range(15):
         wait(mine_kv, kvs.at[i])
@@ -600,11 +653,16 @@
     for i, lanes, sem, _ in moves:
         wait(zs.at[i, :, lanes], z1s.at[sem])
 
+    for i in range(15):
+        wait(slots.at[0, 0:MAIN, :], dis.at[i])
+
     def drain(n, carry):
-        for i, rows in enumerate((MAIN, MAIN, MAIN, 64, 64)):
-            wait(slots.at[0, 0:rows, :], ags.at[i, n])
-
-        @pl.when(n < AG_RELAYED)
+        @pl.when(n > 0)
+        def _():
+            for i, rows in enumerate((MAIN, MAIN, MAIN, 64, 64)):
+                wait(slots.at[0, 0:rows, :], ags.at[i, n])
+
+        @pl.when((n > 0) & (n < AG_RELAYED))
         def _():
             wait(slots.at[0, 0:32, :], ags.at[5, n])
             wait(slots.at[0, 0:32, :], ags.at[6, n])
@@ -638,6 +696,27 @@
     lax.fori_loop(0, NZ, drain, 0)
     for i in range(6):
         wait(scales.at[0:8, :] if i < 3 else scales.at[0:32, :], scs.at[i])
+    mix_copy.wait()
+
+
+def hand_on(att_in, mix_in, att_out, mix_out, att_near, mix_near, sem):
+    parts = [(mix_in, mix_near, mix_out, slice(0, TOK))]
+    parts += [(att_in, att_near, att_out, slice(at, at + MAIN)) for at in range(0, TOK, MAIN)]
+    ins = [
+        pltpu.make_async_copy(src.at[rows, :], near.at[rows, :], sem.at[0, i])
+        for i, (src, near, _, rows) in enumerate(parts)
+    ]
+    outs = [
+        pltpu.make_async_copy(near.at[rows, :], dst.at[rows, :], sem.at[1, i])
+        for i, (_, near, dst, rows) in enumerate(parts)
+    ]
+    for copy in ins:
+        copy.start()
+    for copy, out in zip(ins, outs):
+        copy.wait()
+        out.start()
+    for out in outs:
+        out.wait()
 
 
 def local(
@@ -645,10 +724,13 @@
     gate_weight, up_weight, down_weight,
 ):
     anywhere = pl.BlockSpec(memory_space=pl.ANY)
-    near = pl.BlockSpec(memory_space=pltpu.VMEM)
     vmem = pltpu.VMEM
     dma = pltpu.SemaphoreType.DMA
     scratch = [
+        vmem((1, D), F32),
+        vmem((NZ, D), BF16),
+        vmem((2, TOK), jnp.int32),
+        vmem((TOK, COLS), BF16),
         vmem((TOK, GROUPS * HEAD), BF16),
         vmem((SEQ, 2 * HEAD), BF16),
         vmem((GROUPS * TOK, HEAD), BF16),
@@ -688,7 +770,7 @@
         vmem((NZ, MAIN, UNIT), BF16),
         vmem((NZ, MAIN, UNIT), BF16),
         vmem((NZ * 2 * MAIN, COLS), BF16),
-        dma((8,)),
+        dma((12,)),
         dma((19,)),
         dma((20,)),
         dma((3,)),
@@ -697,6 +779,8 @@
         dma((8,)),
         dma((8,)),
         dma((8,)),
+        dma((15,)),
+        dma((16,)),
         dma((8,)),
         dma((8,)),
         dma((8,)),
@@ -711,14 +795,14 @@
         dma((8,)),
         dma((NZ,)),
     ]
-    return pl.pallas_call(
+    results = pl.pallas_call(
         kernel,
         out_shape=(
             jax.ShapeDtypeStruct((TOK, D), BF16),
             jax.ShapeDtypeStruct((TOK, COLS), BF16),
         ),
-        in_specs=[anywhere] * 5 + [near] * 3 + [anywhere] * 3,
-        out_specs=(anywhere, near),
+        in_specs=[anywhere] * 11,
+        out_specs=(anywhere, anywhere),
         scratch_shapes=scratch,
         compiler_params=pltpu.CompilerParams(
             collective_id=0, has_side_effects=True, vmem_limit_bytes=56 * 1024 * 1024
@@ -737,6 +821,15 @@
         jnp.swapaxes(up_weight, 1, 2),
         down_weight,
     )
+    return pl.pallas_call(
+        hand_on,
+        out_shape=tuple(jax.ShapeDtypeStruct(r.shape, r.dtype) for r in results),
+        in_specs=[anywhere] * 2,
+        out_specs=(anywhere, anywhere),
+        scratch_shapes=[vmem((TOK, D), BF16), vmem((TOK, COLS), BF16), dma((2, 5))],
+        compiler_params=pltpu.CompilerParams(vmem_limit_bytes=60 * 1024 * 1024),
+        name="hand_on",
+    )(*results)
 
 
 def solution(mesh):

time: 93.6 us -> 88.2 us (0.942)
  local copies, waits for them, and re-layouts: 3.34 us -> 0 us
  Pallas kernels: 89.3 us -> 86.7 us
    pallas_call x1, Pallas kernels: 89.3 us -> 84.9 us  [local(): pl.pallas_call(kernel, out_shape=(jax.ShapeDtypeStruct((TOK, D), BF16), j...]
    unnamed x2 -> x0, local copies, waits for them, and re-layouts: 3.34 us -> none
    pallas_call x0 -> x1, Pallas kernels: none -> 1.87 us  [local(): pl.pallas_call(hand_on, out_shape=tuple((jax.ShapeDtypeStruct(r.shape, r....]
where the time goes in v3:
time: 88.2 us; the launch traced here: 87.4 us
  Pallas kernels  86.7 us (98%)
    pallas_call x1, Pallas kernels, local(): pl.pallas_call(kernel, out_shape=(jax.ShapeDtypeStruct((TOK, D), BF16), j...  84.9 us
    pallas_call x1, Pallas kernels, local(): pl.pallas_call(hand_on, out_shape=tuple((jax.ShapeDtypeStruct(r.shape, r....  1.87 us

profile of v3, /device:TPU:8, one launch (start us, length us, event | category | flops | bytes accessed | tf_op | source)
XLA Modules:
  0.0 87.4 jit_solution(1176945246452901999)
XLA Ops:
  0.6 84.9 %layer.1 = (bf16[64,4096]{1,0:T(8,128)(2,1)}, bf16[64,512]{1,0:T(8,128)(2,1)}) custom-call(bf16[64,512]{1,0:T(8,128)(2,1)} %q_ref.1, bf16[64,128]{1,0:T(8,128)(2,1)} %k_ref.1, bf16[64,128]{1,0:T(8,128)(2,1)} %v_ref.1, bf16[64,4096]{1,0:T(8,128)(2,1)} %res_ref.1, bf16[512,4096]{1,0:T(8,128)(2,1)} %wo_ref.1, f32[1,4096]{1,0:T(1,128)} %bitcast.8, ...), custom_call_target="tpu_custom_call" | custom-call | tf_op jit(solution)/shard_map/layer/pallas_call | solution.py:798
  85.5 1.9 %hand_on.1 = (bf16[64,4096]{1,0:T(8,128)(2,1)}, bf16[64,512]{1,0:T(8,128)(2,1)}) custom-call(bf16[64,4096]{1,0:T(8,128)(2,1)} %get-tuple-element.4.att_in, bf16[64,512]{1,0:T(8,128)(2,1)} %get-tuple-element.5.mix_in), custom_call_target="tpu_custom_call" | custom-call | tf_op jit(solution)/shard_map/hand_on/pallas_call | solution.py:824

commit v4 on v3

--- a/solution.py
+++ b/solution.py
@@ -31,7 +31,7 @@
 NT = (((1,), (1,)), ((), ()))
 
 RS_LAGS = (3, 6, 9)
-AG_RELAYED = 8
+AG_RELAYED = 7
 RS_RELAYED = 8
 
 
@@ -327,10 +327,9 @@
                 device = (ctx_of(*at_step(da, 0)), chunk(s))
                 remote(src, dst, ags.at[i, n], agr.at[i, n], device).start()
     slots[e, mine_rows, :] = zunits[e]
-    for i, (da, db) in enumerate(steps):
-        device = (ctx_of(*at_step(da, db)), e)
-        here = slots.at[e, mine_rows, :]
-        remote(here, here, dis.at[i], dir_.at[db * 4 + da], device).start()
+    here = slots.at[e, mine_rows, :]
+    for da, i in first_steps:
+        remote(here, here, ags.at[i, 0], agr.at[i, 0], (ctx_of(*at_step(da, 0)), e)).start()
     squares = jnp.sum(value * value, axis=1, keepdims=True)
     stats[e, 0:NZ, 0:TOK] = lax.dot_general(
         rt_ref[:, cols(e)], scaled, NT, preferred_element_type=F32
@@ -406,7 +405,7 @@
 
     def ag_second(n):
         j = ag_chunk(n)
-        if isinstance(n, int) and n < 3:
+        if isinstance(n, int) and 0 < n < 3:
             wait(slots.at[j, mine_rows, :], zar.at[n])
         wait(slots.at[j, unit(am, b), :], agr.at[0, n])
         wait(slots.at[j, unit(ap, b), :], agr.at[1, n])
@@ -432,13 +431,7 @@
     def ag_use(n):
         j = ag_chunk(n)
 
-        @pl.when(n == 0)
-        def _():
-            for da, db in steps:
-                rows = unit(lax.rem(a + 4 - da, 4), lax.rem(b + 4 - db, 4))
-                wait(slots.at[j, rows, :], dir_.at[db * 4 + da])
-
-        @pl.when((n > 0) & (n < AG_RELAYED))
+        @pl.when(n < AG_RELAYED)
         def _():
             wait(slots.at[j, first_half(b2), :], agr.at[5, n])
             wait(slots.at[j, second_half(b2), :], agr.at[6, n])
@@ -473,6 +466,7 @@
         lax.fori_loop(0, count + last, tick, 0)
 
     stats_send()
+    ag_second(0)
     ag_second(1)
     ag_start(3)
     ag_start(4)
@@ -480,13 +474,16 @@
     ag_start(5)
     ag_start(6)
     ag_start(7)
+    ag_third(0)
     ag_second(3)
     ag_third(1)
     ag_second(4)
+    ag_second(5)
     ag_third(2)
-    ag_second(5)
     ag_second(6)
+    ag_third(3)
     ag_second(7)
+    ag_third(4)
     scale_start()
     columns_send()
 
@@ -495,9 +492,9 @@
     wait(wg.at[FF : 2 * FF], wr.at[0])
     wait(wu.at[FF : 2 * FF], wr.at[1])
     def ag_tick(n, carry):
-        @pl.when((n > 0) & (n + 2 < AG_RELAYED))
-        def _():
-            ag_third(n + 2)
+        @pl.when(n + 5 < AG_RELAYED)
+        def _():
+            ag_third(n + 5)
 
         ag_use(n)
 
@@ -550,12 +547,6 @@
             remote(part.at[n, bundle(b2), :], r2x.at[n], rss.at[0, n], rsr.at[0, n], to_b2).start()
             remote(part.at[n, bundle(bp), :], r2p.at[n], rss.at[2, n], rsr.at[2, n], to_bp).start()
             remote(part.at[n, bundle(bm), :], r2m.at[n], rss.at[3, n], rsr.at[3, n], to_bm).start()
-
-        @pl.when(n > 0)
-        def _():
-            wait(att.at[ag_chunk(n)], atr.at[n])
-
-        out_copy(ag_chunk(n)).start()
 
         @pl.when(n == 7)
         def _():
@@ -594,6 +585,11 @@
             remote(part.at[n, bundle(bm), :], r2m.at[n], rss.at[3, n], rsr.at[3, n], to_bm).start()
 
     def rs_second(n):
+        @pl.when(n > 0)
+        def _():
+            wait(att.at[ag_chunk(n)], atr.at[n])
+
+        out_copy(ag_chunk(n)).start()
         wait(r2p.at[n], rsr.at[2, n])
         wait(r2m.at[n], rsr.at[3, n])
         rows = bundle(b)
@@ -626,7 +622,7 @@
             fin[e] = zout[7]
 
     run(((rs_start, 0),), NZ)
-    run(((rs_last, 10), (rs_second, 6), (rs_first, 0)), NZ)
+    run(((rs_last, 12), (rs_second, 7), (rs_first, 0)), NZ)
 
     for n in range(1, NZ):
         wait(fin.at[ag_chunk(n)], z2r.at[n])
@@ -653,16 +649,12 @@
     for i, lanes, sem, _ in moves:
         wait(zs.at[i, :, lanes], z1s.at[sem])
 
-    for i in range(15):
-        wait(slots.at[0, 0:MAIN, :], dis.at[i])
 
     def drain(n, carry):
-        @pl.when(n > 0)
-        def _():
-            for i, rows in enumerate((MAIN, MAIN, MAIN, 64, 64)):
-                wait(slots.at[0, 0:rows, :], ags.at[i, n])
-
-        @pl.when((n > 0) & (n < AG_RELAYED))
+        for i, rows in enumerate((MAIN, MAIN, MAIN, 64, 64)):
+            wait(slots.at[0, 0:rows, :], ags.at[i, n])
+
+        @pl.when(n < AG_RELAYED)
         def _():
             wait(slots.at[0, 0:32, :], ags.at[5, n])
             wait(slots.at[0, 0:32, :], ags.at[6, n])
@@ -701,7 +693,7 @@
 
 def hand_on(att_in, mix_in, att_out, mix_out, att_near, mix_near, sem):
     parts = [(mix_in, mix_near, mix_out, slice(0, TOK))]
-    parts += [(att_in, att_near, att_out, slice(at, at + MAIN)) for at in range(0, TOK, MAIN)]
+    parts += [(att_in, att_near, att_out, slice(at, at + 32)) for at in range(0, TOK, 32)]
     ins = [
         pltpu.make_async_copy(src.at[rows, :], near.at[rows, :], sem.at[0, i])
         for i, (src, near, _, rows) in enumerate(parts)

time: 88.2 us -> 86.4 us (0.980)
  Pallas kernels: 86.7 us -> 85.6 us
    pallas_call x1, Pallas kernels: 84.9 us -> 83.8 us  [local(): pl.pallas_call(kernel, out_shape=(jax.ShapeDtypeStruct((TOK, D), BF16), j...]
where the time goes in v4:
time: 86.4 us; the launch traced here: 86.3 us
  Pallas kernels  85.6 us (99%)
    pallas_call x1, Pallas kernels, local(): pl.pallas_call(kernel, out_shape=(jax.ShapeDtypeStruct((TOK, D), BF16), j...  83.8 us
    pallas_call x1, Pallas kernels, local(): pl.pallas_call(hand_on, out_shape=tuple((jax.ShapeDtypeStruct(r.shape, r....  1.87 us

profile of v4, /device:TPU:8, one launch (start us, length us, event | category | flops | bytes accessed | tf_op | source)
XLA Modules:
  0.0 86.3 jit_solution(11377731226767280131)
XLA Ops:
  0.6 83.8 %layer.1 = (bf16[64,4096]{1,0:T(8,128)(2,1)}, bf16[64,512]{1,0:T(8,128)(2,1)}) custom-call(bf16[64,512]{1,0:T(8,128)(2,1)} %q_ref.1, bf16[64,128]{1,0:T(8,128)(2,1)} %k_ref.1, bf16[64,128]{1,0:T(8,128)(2,1)} %v_ref.1, bf16[64,4096]{1,0:T(8,128)(2,1)} %res_ref.1, bf16[512,4096]{1,0:T(8,128)(2,1)} %wo_ref.1, f32[1,4096]{1,0:T(1,128)} %bitcast.8, ...), custom_call_target="tpu_custom_call" | custom-call | tf_op jit(solution)/shard_map/layer/pallas_call | solution.py:790
  84.4 1.9 %hand_on.1 = (bf16[64,4096]{1,0:T(8,128)(2,1)}, bf16[64,512]{1,0:T(8,128)(2,1)}) custom-call(bf16[64,4096]{1,0:T(8,128)(2,1)} %get-tuple-element.4.att_in, bf16[64,512]{1,0:T(8,128)(2,1)} %get-tuple-element.5.mix_in), custom_call_target="tpu_custom_call" | custom-call | tf_op jit(solution)/shard_map/hand_on/pallas_call | solution.py:816

commit v5 on v4

--- a/solution.py
+++ b/solution.py
@@ -603,9 +603,9 @@
             wait(r2x.at[n], rsr.at[0, n])
             part[n, rows, every] = add(n, rows, every, [r2p[n], r2m[n], r2x[n]]).astype(BF16)
 
-        remote(part.at[n, unit(a2, b), :], r4x.at[n], rss.at[4, n], rsr.at[4, n], to_a2).start()
         remote(part.at[n, unit(ap, b), :], r4p.at[n], rss.at[5, n], rsr.at[5, n], to_ap).start()
         remote(part.at[n, unit(am, b), :], r4m.at[n], rss.at[6, n], rsr.at[6, n], to_am).start()
+        remote(part.at[n, unit(a2, b), :], r4x.at[n], rss.at[4, n], rsr.at[4, n], to_a2).start()
 
     def rs_last(n):
         wait(r4p.at[n], rsr.at[5, n])

time: 86.4 us -> 86.6 us (level)
  no operation moved by 1% of the time
where the time goes in v5:
time: 86.6 us; the launch traced here: 86.5 us
  Pallas kernels  85.8 us (99%)
    pallas_call x1, Pallas kernels, local(): pl.pallas_call(kernel, out_shape=(jax.ShapeDtypeStruct((TOK, D), BF16), j...  84 us
    pallas_call x1, Pallas kernels, local(): pl.pallas_call(hand_on, out_shape=tuple((jax.ShapeDtypeStruct(r.shape, r....  1.87 us

profile of v5, /device:TPU:8, one launch (start us, length us, event | category | flops | bytes accessed | tf_op | source)
XLA Modules:
  0.0 86.5 jit_solution(15340274499924013109)
XLA Ops:
  0.6 84.0 %layer.1 = (bf16[64,4096]{1,0:T(8,128)(2,1)}, bf16[64,512]{1,0:T(8,128)(2,1)}) custom-call(bf16[64,512]{1,0:T(8,128)(2,1)} %q_ref.1, bf16[64,128]{1,0:T(8,128)(2,1)} %k_ref.1, bf16[64,128]{1,0:T(8,128)(2,1)} %v_ref.1, bf16[64,4096]{1,0:T(8,128)(2,1)} %res_ref.1, bf16[512,4096]{1,0:T(8,128)(2,1)} %wo_ref.1, f32[1,4096]{1,0:T(1,128)} %bitcast.8, ...), custom_call_target="tpu_custom_call" | custom-call | tf_op jit(solution)/shard_map/layer/pallas_call | solution.py:790
  84.6 1.9 %hand_on.1 = (bf16[64,4096]{1,0:T(8,128)(2,1)}, bf16[64,512]{1,0:T(8,128)(2,1)}) custom-call(bf16[64,4096]{1,0:T(8,128)(2,1)} %get-tuple-element.4.att_in, bf16[64,512]{1,0:T(8,128)(2,1)} %get-tuple-element.5.mix_in), custom_call_target="tpu_custom_call" | custom-call | tf_op jit(solution)/shard_map/hand_on/pallas_call | solution.py:816
